TPU v7x, 512 devices: a whole 4x8x8 slice. The times are simulated.
512 devices in a mesh: head: 8 (over y_lo, core), ctx: 64 (over z, x, y_hi).
Axes of the slice: x: 4, y: 8 (y_hi: 2, y_lo: 4; y = y_hi * 4 + y_lo), z: 8, core: 2. Of those that a mesh axis runs over, the one named last changes fastest.
Arguments:
- queries: bfloat16 [12288, 2048], P(('head', 'ctx')), may hold values from -40 to 40
- keys: bfloat16 [12288, 2048], P(('head', 'ctx')), may hold values from -8 to 8
- values: bfloat16 [12288, 2048], P(('head', 'ctx')), may hold values from -6 to 6
Outputs:
- attended: bfloat16 [12288, 2048], P(('head', 'ctx'))
All inputs are finite; a program needn't handle non-finite values.
Results may differ from a plain program's by a relative error of at most 0.0095.
Values may be sent and summed in bfloat16 or wider, within the bound.
No kernel may reach another device: no remote copies, remote signals or barrier semaphores. Data moves between devices by JAX's collectives and lax.ppermute only.
A program may use at most 64 MiB of HBM per device.

v0:
```python
import math

import jax
import jax.numpy as jnp
from jax import lax
from jax.sharding import PartitionSpec as P

HD = 128


def fold_block(query_block, running, key_block, value_block):
    running_max, running_sum, numerator = running
    scores = jnp.einsum("hqd,hkd->hqk", query_block, key_block, preferred_element_type=jnp.float32)
    scores = scores * (1.0 / math.sqrt(HD))
    new_max = jnp.maximum(running_max, jnp.max(scores, axis=2))
    weights = jnp.exp(scores - new_max[:, :, None])
    factor = jnp.exp(running_max - new_max)
    new_sum = running_sum * factor + jnp.sum(weights, axis=2)
    added = jnp.einsum(
        "hqk,hkd->hqd",
        weights.astype(jnp.bfloat16),
        value_block,
        preferred_element_type=jnp.float32,
    )
    new_numerator = numerator * factor[:, :, None] + added
    return (new_max, new_sum, new_numerator)


def fold_step(query_block, running, block_pair):
    key_piece, value_piece = block_pair
    head_count = key_piece.shape[0]
    key_rows = key_piece.shape[1]
    block_rows = math.gcd(key_rows, 512)
    count = key_rows // block_rows
    shape = (head_count, count, block_rows, key_piece.shape[2])
    key_blocks = jnp.moveaxis(key_piece.reshape(shape), 1, 0)
    value_blocks = jnp.moveaxis(value_piece.reshape(shape), 1, 0)

    def inner(carry, pair):
        return (fold_block(query_block, carry, pair[0], pair[1]), None)

    running, unused = lax.scan(inner, running, (key_blocks, value_blocks))
    return running


def start_state(query_rows, head_count):
    return (
        jnp.full((head_count, query_rows), -jnp.inf, jnp.float32),
        jnp.zeros((head_count, query_rows), jnp.float32),
        jnp.zeros((head_count, query_rows, HD), jnp.float32),
    )


def finish(running):
    running_max, running_sum, numerator = running
    return numerator / running_sum[:, :, None]


def per_device(queries, keys, values):
    token_rows = queries.shape[0]
    head_total = queries.shape[1] // HD

    def reshape_heads(array):
        return array.reshape(token_rows, head_total, HD)

    local_q, local_k, local_v = (
        lax.all_to_all(reshape_heads(queries), "head", split_axis=1, concat_axis=0, tiled=True),
        lax.all_to_all(reshape_heads(keys), "head", split_axis=1, concat_axis=0, tiled=True),
        lax.all_to_all(reshape_heads(values), "head", split_axis=1, concat_axis=0, tiled=True),
    )
    query_rows = local_q.shape[0]
    heads_q = local_q.transpose(1, 0, 2)
    heads_k = local_k.transpose(1, 0, 2)
    heads_v = local_v.transpose(1, 0, 2)

    def one_head(triple):
        query_head, key_head, value_head = triple
        query_block = query_head[None]
        running = fold_step(
            query_block,
            start_state(query_rows, 1),
            (
                lax.all_gather(key_head[None], "ctx", axis=1, tiled=True),
                lax.all_gather(value_head[None], "ctx", axis=1, tiled=True),
            ),
        )
        return finish(running)[0]

    output = lax.map(one_head, (heads_q, heads_k, heads_v))
    rounded = output.astype(jnp.bfloat16).transpose(1, 0, 2)
    returned = lax.all_to_all(rounded, "head", split_axis=0, concat_axis=1, tiled=True)
    return returned.reshape(token_rows, head_total * HD)


def solution(mesh):
    placed = (P(("head", "ctx"), None), P(("head", "ctx"), None), P(("head", "ctx"), None))
    return jax.shard_map(
        per_device, mesh=mesh, in_specs=placed, out_specs=P(("head", "ctx"), None), check_vma=False
    )
```

profile of v0, /device:TPU:1, one launch (start us, length us, event | category | flops | bytes accessed | tf_op | source)
XLA Modules:
  0.0 775.3 jit_solution(10254957134040522212)
XLA Ops:
  8.1 10.1 %all-to-all-start.1 = ((bf16[24,16,128]{2,0,1:T(8,128)(2,1)}), bf16[24,16,128]{2,0,1:T(8,128)(2,1)S(1)}, u32[]{:S(2)}, u32[]{:S(2)}) async-start(bf16[24,16,128]{2,0,1:T(8,128)(2,1)} %copy_bitcast_fusion.1), calls=%async_computation.1 | async-start | bytes 196608 | tf_op jit(solution)/shard_map/all_to_all | solution.py:69
  18.2 1.5 copy_bitcast_fusion
  19.8 4.0 all-to-all-done.1
  23.7 4.1 all-to-all-start.2
  27.9 1.5 copy_bitcast_fusion.2
  29.4 4.0 all-to-all-done.2
  33.4 4.1 all-to-all-start
  37.5 5.5 all-to-all-done
  43.0 709.6 %while.26 = (s32[]{:T(128)}, bf16[2,192,128]{2,0,1:T(2,128)(2,1)S(1)}, bf16[2,192,128]{2,1,0:T(8,128)(2,1)S(1)}, bf16[2,192,128]{2,1,0:T(8,128)(2,1)S(1)}, bf16[...) while((s32[]{:T(128)}, bf16[2,192,128]{2,0,1:T(2,128)(2,1)S(1)}, ...), condition=%wide.region_5.6_spmd, body=%wide.region_0.5_spmd.sunk | while | flops 51020736 | bytes 21559420 | solution.py:89
  44.6 142.6 %all-gather.3.cloned.1.call-done = bf16[1,12288,128]{2,1,0:T(8,128)(2,1)} async-done(((bf16[1,192,128]{2,1,0:T(8,128)(2,1)}), bf16[1,12288,128]{2,1,0:T(8,128)(2,1)}) %all-gather.3.cloned.1.call-update) | async-done | bytes 3145744 | tf_op jit(solution)/shard_map/while/body/eval_jaxpr/all_gather | solution.py:83
  187.2 143.9 %all-gather.5.cloned.1.call-done = bf16[1,12288,128]{2,1,0:T(8,128)(2,1)} async-done(((bf16[1,192,128]{2,1,0:T(8,128)(2,1)}), bf16[1,12288,128]{2,1,0:T(8,128)(2,1)}) %all-gather.5.cloned.1.call-update) | async-done | bytes 3145744 | tf_op jit(solution)/shard_map/while/body/eval_jaxpr/all_gather | solution.py:84
  331.0 64.1 %while.27 = (s32[]{:T(128)}, f32[1,192]{1,0:T(1,128)S(1)}, f32[1,192]{1,0:T(1,128)S(1)}, f32[1,192,128]{2,1,0:T(8,128)S(1)}, bf16[24,1,512,128]{3,2,1,0:T(8,128)...) while((s32[]{:T(128)}, f32[1,192]{1,0:T(1,128)S(1)}, ...), condition=%wide.region_4.4_spmd.clone, body=%wide.region_1.3_spmd.clone.sunk | while | flops 50996160 | bytes 1700969 | solution.py:42
  331.0 1.2 fusion.28
  333.7 1.2 fusion.28
  336.4 1.2 fusion.28
  339.0 1.2 fusion.28
  341.7 1.2 fusion.28
  344.4 1.2 fusion.28
  347.1 1.2 fusion.28
  349.7 1.2 fusion.28
  352.4 1.2 fusion.28
  355.1 1.2 fusion.28
  357.7 1.2 fusion.28
  360.4 1.2 fusion.28
  363.1 1.2 fusion.28
  365.7 1.2 fusion.28
  368.4 1.2 fusion.28
  371.1 1.2 fusion.28
  373.8 1.2 fusion.28
  376.4 1.2 fusion.28
  379.1 1.2 fusion.28
  381.8 1.2 fusion.28
  384.4 1.2 fusion.28
  387.1 1.2 fusion.28
  389.8 1.2 fusion.28
  392.4 1.2 fusion.28
  395.2 2.4 dynamic_update_slice.5
  399.1 143.2 %all-gather.3.cloned.1.call-done = bf16[1,12288,128]{2,1,0:T(8,128)(2,1)} async-done(((bf16[1,192,128]{2,1,0:T(8,128)(2,1)}), bf16[1,12288,128]{2,1,0:T(8,128)(2,1)}) %all-gather.3.cloned.1.call-update) | async-done | bytes 3145744 | tf_op jit(solution)/shard_map/while/body/eval_jaxpr/all_gather | solution.py:83
  542.3 143.7 %all-gather.5.cloned.1.call-done = bf16[1,12288,128]{2,1,0:T(8,128)(2,1)} async-done(((bf16[1,192,128]{2,1,0:T(8,128)(2,1)}), bf16[1,12288,128]{2,1,0:T(8,128)(2,1)}) %all-gather.5.cloned.1.call-update) | async-done | bytes 3145744 | tf_op jit(solution)/shard_map/while/body/eval_jaxpr/all_gather | solution.py:84
  686.0 64.0 %while.27 = (s32[]{:T(128)}, f32[1,192]{1,0:T(1,128)S(1)}, f32[1,192]{1,0:T(1,128)S(1)}, f32[1,192,128]{2,1,0:T(8,128)S(1)}, bf16[24,1,512,128]{3,2,1,0:T(8,128)...) while((s32[]{:T(128)}, f32[1,192]{1,0:T(1,128)S(1)}, ...), condition=%wide.region_4.4_spmd.clone, body=%wide.region_1.3_spmd.clone.sunk | while | flops 50996160 | bytes 1700969 | solution.py:42
  688.7 1.2 fusion.28
  691.4 1.2 fusion.28
  694.0 1.2 fusion.28
  696.7 1.2 fusion.28
  699.4 1.2 fusion.28
  702.0 1.2 fusion.28
  704.7 1.2 fusion.28
  707.4 1.2 fusion.28
  710.1 1.2 fusion.28
  712.7 1.2 fusion.28
  715.4 1.2 fusion.28
  718.1 1.2 fusion.28
  720.7 1.2 fusion.28
  723.4 1.2 fusion.28
  726.1 1.2 fusion.28
  728.7 1.2 fusion.28
  731.4 1.2 fusion.28
  734.1 1.2 fusion.28
  736.7 1.2 fusion.28
  742.1 1.2 fusion.28
  744.8 1.2 fusion.28
  747.4 1.2 fusion.28
  750.2 2.4 dynamic_update_slice.5
  752.6 15.4 %all_to_all.69 = bf16[192,2,128]{2,1,0:T(2,128)(2,1)S(1)} all-to-all(bf16[192,2,128]{2,1,0:T(2,128)(2,1)S(1)} %bitcast.104), channel_id=1, replica_groups=mesh['head'=8,'ctx'=64] {'head'}, dimensions={0} | all-to-all | bytes 196608 | tf_op jit(solution)/shard_map/all_to_all | solution.py:91
  (273 shorter events, 75.7 us)
Async XLA Ops:
  6.5 0.9 copy-start
  8.1 15.6 %all-to-all-start.1 = ((bf16[24,16,128]{2,0,1:T(8,128)(2,1)}), bf16[24,16,128]{2,0,1:T(8,128)(2,1)S(1)}, u32[]{:S(2)}, u32[]{:S(2)}) async-start(bf16[24,16,128]{2,0,1:T(8,128)(2,1)} %copy_bitcast_fusion.1), calls=%async_computation.1 | async-start | bytes 196608 | tf_op jit(solution)/shard_map/all_to_all | solution.py:69
  23.7 9.6 %all-to-all-start.2 = ((bf16[24,16,128]{2,0,1:T(8,128)(2,1)}), bf16[24,16,128]{2,0,1:T(8,128)(2,1)S(1)}, u32[]{:S(2)}, u32[]{:S(2)}) async-start(bf16[24,16,128]{2,0,1:T(8,128)(2,1)} %copy_bitcast_fusion), calls=%async_computation.2 | async-start | bytes 196608 | tf_op jit(solution)/shard_map/all_to_all | solution.py:67
  33.4 9.6 %all-to-all-start = ((bf16[24,16,128]{2,0,1:T(8,128)(2,1)}), bf16[24,16,128]{2,0,1:T(8,128)(2,1)S(1)}, u32[]{:S(2)}, u32[]{:S(2)}) async-start(bf16[24,16,128]{2,0,1:T(8,128)(2,1)} %copy_bitcast_fusion.2), calls=%async_computation | async-start | bytes 196608 | tf_op jit(solution)/shard_map/all_to_all | solution.py:68
  43.0 144.1 %all-gather.3.cloned.1.call-start = ((), (), s32[]{:S(2)}) async-start(), calls=%async_computation.4 | async-start | bytes 3194880 | tf_op jit(solution)/shard_map/while/body/eval_jaxpr/all_gather | solution.py:83
  43.8 287.3 %all-gather.5.cloned.1.call-start = ((), (), s32[]{:S(2)}) async-start(), calls=%async_computation.5 | async-start | bytes 3194880 | tf_op jit(solution)/shard_map/while/body/eval_jaxpr/all_gather | solution.py:84
  397.6 144.7 %all-gather.3.cloned.1.call-start = ((), (), s32[]{:S(2)}) async-start(), calls=%async_computation.4 | async-start | bytes 3194880 | tf_op jit(solution)/shard_map/while/body/eval_jaxpr/all_gather | solution.py:83
  398.4 287.7 %all-gather.5.cloned.1.call-start = ((), (), s32[]{:S(2)}) async-start(), calls=%async_computation.5 | async-start | bytes 3194880 | tf_op jit(solution)/shard_map/while/body/eval_jaxpr/all_gather | solution.py:84
Sparse Core Ops, SparseCore 0:
  48.4 138.7 all-gather.2
  191.7 139.2 all-gather.4
  403.0 139.2 all-gather.2
  546.7 139.2 all-gather.4
where the time goes:
time: 777 us; the launch traced here: 775 us
  waiting for transfers between devices  587 us (76%)
  matrix products  114 us (15%)
  starting transfers between devices  18.6 us (2%)
  blocking collectives  15.4 us (2%)
  between operations  13.1 us (2%)
  local copies, waits for them, and re-layouts  12.9 us (2%)
  other arithmetic  11.6 us (1%)
    all_gather x2, waiting for transfers between devices, one_head(): lax.all_gather(value_head[None], 'ctx', axis=1, tiled=True)  288 us
    all_gather x2, waiting for transfers between devices, one_head(): lax.all_gather(key_head[None], 'ctx', axis=1, tiled=True)  286 us
    dot_general x48, matrix products, fold_block(): jnp.einsum('hqd,hkd->hqk', query_block, key_block, preferred_element_type...  58 us
    dot_general x48, matrix products, fold_block(): jnp.einsum('hqk,hkd->hqd', weights.astype(jnp.bfloat16), value_block, pre...  56.4 us
  transfers between devices with their start and end apart: 7, of which 7 were waited for; matrix products, arithmetic and copies ran while one was open for 1% of the time, Pallas kernels for 0%

commit v1 on v0

v1 whole, which is shorter than its diff:
```python
import functools
import math

import jax
import jax.numpy as jnp
from jax import lax
from jax.experimental import pallas as pl
from jax.experimental.pallas import tpu as pltpu
from jax.sharding import Mesh, PartitionSpec as P

HD = 128
HEADS = 16
TOKENS = 24
SIDE = 8
SCALE = math.log2(math.e) / math.sqrt(HD)
VMEM = pltpu.CompilerParams(vmem_limit_bytes=48 * 1024 * 1024)

AXES = ("yl", "c", "zh", "zl", "x", "yh")
SIZES = (4, 2, 4, 2, 4, 2)
HEAD_GROUP = ("yh", "yl", "zl")
BACK_GROUP = ("zh", "yh", "yl", "zl")


def whole(count):
    return [pl.BlockSpec(memory_space=pltpu.VMEM)] * count


def pack_kernel(q_ref, k_ref, v_ref, out_ref):
    for head in range(HEADS):
        columns = slice(head * HD, (head + 1) * HD)
        out_ref[head, :, 0:HD] = q_ref[:, columns]
        out_ref[head, :, HD : 2 * HD] = k_ref[:, columns]
        out_ref[head, :, 2 * HD : 3 * HD] = v_ref[:, columns]


def pack(queries, keys, values):
    return pl.pallas_call(
        pack_kernel,
        out_shape=jax.ShapeDtypeStruct((HEADS, TOKENS, 3 * HD), jnp.bfloat16),
        in_specs=whole(3),
        out_specs=pl.BlockSpec(memory_space=pltpu.VMEM),
        compiler_params=VMEM,
        name="pack",
    )(queries, keys, values)


def attend_kernel(q_ref, kv0_ref, kv1_ref, out_ref, keys_ref, wide_ref, scores_ref, *, rows):
    half = kv0_ref.shape[0]
    for part, kv_ref in enumerate((kv0_ref, kv1_ref)):
        span = slice(part * half, (part + 1) * half)
        keys_ref[span, :] = kv_ref[:, :HD]
        wide_ref[span, :HD] = kv_ref[:, HD:]
    wide_ref[:, HD:] = jnp.ones((2 * half, HD), jnp.bfloat16)
    count = q_ref.shape[0] // rows
    blocks = rows // TOKENS
    lane = lax.broadcasted_iota(jnp.int32, (blocks, SIDE, HD), 2)

    def scores(step):
        return lax.dot_general(
            q_ref[step * rows : (step + 1) * rows, :],
            keys_ref[...],
            (((1,), (1,)), ((), ())),
            preferred_element_type=jnp.float32,
        )

    def finish(step, tile):
        top = jnp.max(tile, axis=1, keepdims=True)
        weights = jnp.exp2((tile - top) * SCALE).astype(jnp.bfloat16)
        sums = jnp.dot(weights, wide_ref[...], preferred_element_type=jnp.float32)
        total = sums[:, HD:]
        share = (sums[:, :HD] / total).reshape(blocks, TOKENS, HD)
        rest = (jnp.log2(total) + top * SCALE).reshape(blocks, TOKENS, HD)
        side = jnp.zeros((blocks, SIDE, HD), jnp.float32)
        for term in range(3):
            piece = rest.astype(jnp.bfloat16).astype(jnp.float32)
            rest = rest - piece
            for group in range(TOKENS // SIDE):
                side = jnp.where(
                    lane == group * 3 + term, piece[:, group * SIDE : (group + 1) * SIDE, :], side
                )
        out_ref[step * blocks : (step + 1) * blocks] = jnp.concatenate([share, side], axis=1).astype(
            jnp.bfloat16
        )

    scores_ref[0] = scores(0)
    for step in range(count):
        if step + 1 < count:
            scores_ref[(step + 1) % 2] = scores(step + 1)
        finish(step, scores_ref[step % 2])


def attend(query, kv0, kv1, rows=192):
    count = query.shape[0]
    half = kv0.shape[0]
    return pl.pallas_call(
        functools.partial(attend_kernel, rows=rows),
        out_shape=jax.ShapeDtypeStruct((count // TOKENS, TOKENS + SIDE, HD), jnp.bfloat16),
        in_specs=whole(3),
        out_specs=pl.BlockSpec(memory_space=pltpu.VMEM),
        scratch_shapes=[
            pltpu.VMEM((2 * half, HD), jnp.bfloat16),
            pltpu.VMEM((2 * half, 2 * HD), jnp.bfloat16),
            pltpu.VMEM((2, rows, 2 * half), jnp.float32),
        ],
        compiler_params=VMEM,
        cost_estimate=pl.CostEstimate(
            flops=8 * count * half * HD, bytes_accessed=4 << 20, transcendentals=2 * count * half
        ),
        name="attend",
    )(query, kv0, kv1)


def combine_kernel(parts_ref, out_ref):
    for head in range(HEADS):
        blocks = [parts_ref[part * HEADS + head].astype(jnp.float32) for part in range(4)]
        for group in range(TOKENS // SIDE):
            rows = slice(group * SIDE, (group + 1) * SIDE)
            logs = []
            for block in blocks:
                side = block[TOKENS:, group * 3 : group * 3 + 3]
                logs.append(side[:, 0:1] + side[:, 1:2] + side[:, 2:3])
            top = jnp.maximum(jnp.maximum(logs[0], logs[1]), jnp.maximum(logs[2], logs[3]))
            factors = [jnp.exp2(log - top) for log in logs]
            total = factors[0] + factors[1] + factors[2] + factors[3]
            acc = blocks[0][rows] * (factors[0] / total)
            for part in range(1, 4):
                acc = acc + blocks[part][rows] * (factors[part] / total)
            out_ref[rows, head * HD : (head + 1) * HD] = acc


def combine(parts):
    return pl.pallas_call(
        combine_kernel,
        out_shape=jax.ShapeDtypeStruct((TOKENS, HEADS * HD), jnp.float32),
        in_specs=whole(1),
        out_specs=pl.BlockSpec(memory_space=pltpu.VMEM),
        compiler_params=VMEM,
        name="combine",
    )(parts)


def shift(axis, by, size):
    return [(source, (source + by) % size) for source in range(size)]


def per_device(queries, keys, values):
    packed = pack(queries, keys, values)
    mine = lax.all_to_all(packed, HEAD_GROUP, split_axis=0, concat_axis=0, tiled=True)
    mine = mine.reshape(HEADS * TOKENS, 3 * HD)
    own_q = mine[:, :HD]
    own_kv = mine[:, HD:]
    others = [lax.ppermute(own_q, "zh", shift("zh", by, 4)) for by in (1, 2, 3)]
    kv = lax.all_to_all(
        jnp.broadcast_to(own_kv[None], (4,) + own_kv.shape), "x", split_axis=0, concat_axis=0, tiled=True
    ).reshape(4 * own_kv.shape[0], 2 * HD)
    other_kv = lax.ppermute(kv, "c", [(0, 1), (1, 0)])
    query = jnp.concatenate([own_q] + others, axis=0)
    parts = attend(query, kv, other_kv)
    me = lax.axis_index("zh")
    slots = parts.reshape(4, HEADS, TOKENS + SIDE, HD)
    slots = jnp.take(slots, (me - jnp.arange(4)) % 4, axis=0)
    sent = lax.all_to_all(
        slots.reshape(parts.shape), BACK_GROUP, split_axis=0, concat_axis=0, tiled=True
    )
    return combine(sent).astype(jnp.bfloat16)


def solution(mesh):
    fine = Mesh(mesh.devices.reshape(SIZES), AXES)
    placed = P(AXES, None)
    return jax.shard_map(
        per_device, mesh=fine, in_specs=(placed,) * 3, out_specs=placed, check_vma=False
    )
```

time: 777 us -> 99.7 us (0.13)
  the two profiles are of different devices: /device:TPU:1 before, /device:TPU:16 now
where the time goes in v1:
time: 99.7 us; the launch traced here: 99.3 us
  blocking collectives  62.1 us (62%)
  starting transfers between devices  19.9 us (20%)
  Pallas kernels  7.29 us (7%)
  waiting for transfers between devices  5.51 us (6%)
  local copies, waits for them, and re-layouts  3.56 us (4%)
    all_to_all x1, blocking collectives, per_device(): lax.all_to_all(slots.reshape(parts.shape), BACK_GROUP, split_axis=0, conc...  27 us
    all_to_all x1, blocking collectives, per_device(): lax.all_to_all(packed, HEAD_GROUP, split_axis=0, concat_axis=0, tiled=True)  19.8 us
    ppermute x3, starting transfers between devices, per_device(): others = [lax.ppermute(own_q, 'zh', shift('zh', by, 4)) for by in (1, 2, 3)]  18 us
    all_to_all x1, blocking collectives, per_device(): lax.all_to_all(jnp.broadcast_to(own_kv[None], (4,) + own_kv.shape), 'x',...  15.3 us
    pallas_call x1, Pallas kernels, attend(): pl.pallas_call(functools.partial(attend_kernel, rows=rows), out_shape=jax...  5.93 us
    ppermute x3, waiting for transfers between devices, per_device(): others = [lax.ppermute(own_q, 'zh', shift('zh', by, 4)) for by in (1, 2, 3)]  5.5 us
    unnamed x6, local copies, waits for them, and re-layouts  2.68 us
  transfers between devices with their start and end apart: 4, of which 2 were waited for; matrix products, arithmetic and copies ran while one was open for 0% of the time, Pallas kernels for 0%

profile of v1, /device:TPU:16, one launch (start us, length us, event | category | flops | bytes accessed | tf_op | source)
XLA Modules:
  0.0 99.3 jit_solution(11822663005951308633)
XLA Ops:
  0.0 0.0 copy-start
  0.0 0.9 copy-done
  0.9 0.0 copy-start.1
  0.9 0.9 copy-done.1
  1.8 0.0 copy-start.2
  1.8 0.9 copy-done.2
  2.7 0.1 pack.1
  2.7 19.8 %all_to_all.15 = bf16[16,24,384]{2,1,0:T(8,128)(2,1)S(1)} all-to-all(bf16[16,24,384]{2,1,0:T(8,128)(2,1)S(1)} %pack.1), channel_id=1, replica_groups=mesh['yl'=4,'c'=2,'zh'=4,'zl'=2,'x'=4,'yh'=2] {'yh','yl','zl'}, dimensions={0} | all-to-all | bytes 589824 | tf_op jit(solution)/shard_map/all_to_all | solution.py:148
  22.6 0.1 broadcast_in_dim.23
  22.6 15.3 %all_to_all.16 = bf16[4,384,256]{2,1,0:T(8,128)(2,1)S(1)} all-to-all(bf16[4,384,256]{2,1,0:T(8,128)(2,1)S(1)} %broadcast_in_dim.23), channel_id=1, replica_groups=mesh['yl'=4,'c'=2,'zh'=4,'zl'=2,'x'=4,'yh'=2] {'x'}, dimensions={0} | all-to-all | bytes 1572864 | tf_op jit(solution)/shard_map/all_to_all | solution.py:153
  37.9 1.9 %collective-permute-start.3 = (bf16[1536,256]{1,0:T(8,128)(2,1)S(1)}, bf16[1536,256]{1,0:T(8,128)(2,1)S(1)}, u32[]{:S(2)}, u32[]{:S(2)}) collective-permute-start(bf16[1536,256]{1,0:T(8,128)(2,1)S(1)} %bitcast.7), channel_id=1, source_target_pairs={{0,64},{64,0},{1,65},{65,1},{2,66},{66,2},{3,67},{67,3},{4,68},{68... | collective-permute-start | bytes 2359304 | tf_op jit(solution)/shard_map/ppermute | solution.py:156
  39.9 0.1 broadcast_in_dim.20
  39.9 0.1 broadcast_in_dim.21
  40.1 6.1 %collective-permute-start = (bf16[384,128]{1,0:T(8,128)(2,1)S(1)}, bf16[384,128]{1,0:T(8,128)(2,1)S(1)}, u32[]{:S(2)}, u32[]{:S(2)}) collective-permute-start(bf16[384,128]{1,0:T(8,128)(2,1)S(1)} %slice.10), channel_id=1, source_target_pairs={{0,16},{16,32},{32,48},{48,0},{1,17},{17,33},{33,49},{49,1},{2,18}... | collective-permute-start | bytes 294920 | tf_op jit(solution)/shard_map/ppermute | solution.py:152
  46.1 8.2 %collective-permute-start.1 = (bf16[384,128]{1,0:T(8,128)(2,1)S(1)}, bf16[384,128]{1,0:T(8,128)(2,1)S(1)}, u32[]{:S(2)}, u32[]{:S(2)}) collective-permute-start(bf16[384,128]{1,0:T(8,128)(2,1)S(1)} %slice.10), channel_id=1, source_target_pairs={{0,32},{16,48},{32,0},{48,16},{1,33},{17,49},{33,1},{49,17},{2,34}... | collective-permute-start | bytes 294920 | tf_op jit(solution)/shard_map/ppermute | solution.py:152
  54.4 3.7 %collective-permute-start.2 = (bf16[384,128]{1,0:T(8,128)(2,1)S(1)}, bf16[384,128]{1,0:T(8,128)(2,1)S(1)}, u32[]{:S(2)}, u32[]{:S(2)}) collective-permute-start(bf16[384,128]{1,0:T(8,128)(2,1)S(1)} %slice.10), channel_id=1, source_target_pairs={{0,48},{16,0},{32,16},{48,32},{1,49},{17,1},{33,17},{49,33},{2,50}... | collective-permute-start | bytes 294920 | tf_op jit(solution)/shard_map/ppermute | solution.py:152
  58.1 0.0 collective-permute-done
  58.1 3.7 %collective-permute-done.1 = bf16[384,128]{1,0:T(8,128)(2,1)S(1)} collective-permute-done((bf16[384,128]{1,0:T(8,128)(2,1)S(1)}, bf16[384,128]{1,0:T(8,128)(2,1)S(1)}, u32[]{:S(2)}, u32[]{:S(2)}) %collective-permute-start.1) | collective-permute-done | bytes 98336 | tf_op jit(solution)/shard_map/ppermute | solution.py:152
  61.8 1.8 %collective-permute-done.2 = bf16[384,128]{1,0:T(8,128)(2,1)S(1)} collective-permute-done((bf16[384,128]{1,0:T(8,128)(2,1)S(1)}, bf16[384,128]{1,0:T(8,128)(2,1)S(1)}, u32[]{:S(2)}, u32[]{:S(2)}) %collective-permute-start.2) | collective-permute-done | bytes 98336 | tf_op jit(solution)/shard_map/ppermute | solution.py:152
  63.6 0.0 collective-permute-done.3.kv1_ref
  63.6 5.9 %attend.1 = bf16[64,32,128]{2,1,0:T(8,128)(2,1)S(1)} custom-call(bf16[1536,128]{1,0:T(8,128)(2,1)S(1)} %pad_maximum_fusion.q_ref, bf16[1536,256]{1,0:T(8,128)(2,1)S(1)} %bitcast.8, bf16[1536,256]{1,0:T(8,128)(2,1)S(1)} %collective-permute-done.3.kv1_ref), custom_call_target="tpu_custom_call" | custom-call | flops 2415919104 | bytes 4194304 | tf_op jit(solution)/shard_map/attend/pallas_call | solution.py:95
  69.5 0.6 gather_fusion
  70.2 0.1 bitcast_select_fusion
  70.3 27.0 %all_to_all.17.parts_ref = bf16[64,32,128]{2,1,0:T(8,128)(2,1)S(1)} all-to-all(bf16[64,32,128]{2,1,0:T(8,128)(2,1)S(1)} %bitcast_select_fusion), channel_id=1, replica_groups=mesh['yl'=4,'c'=2,'zh'=4,'zl'=2,'x'=4,'yh'=2] {'zh','yh','yl','zl'}, dimensions={0} | all-to-all | bytes 1048576 | tf_op jit(solution)/shard_map/all_to_all | solution.py:162
  97.3 1.3 %combine.1 = f32[24,2048]{1,0:T(8,128)S(1)} custom-call(bf16[64,32,128]{2,1,0:T(8,128)(2,1)S(1)} %all_to_all.17.parts_ref), custom_call_target="tpu_custom_call" | custom-call | tf_op jit(solution)/shard_map/combine/pallas_call | solution.py:132
  98.6 0.7 convert_element_type.3
  (6 shorter events, 0.1 us)
Async XLA Ops:
  0.0 0.9 copy-start
  0.9 0.9 copy-start.1
  1.8 0.9 copy-start.2
  37.9 25.7 %collective-permute-start.3 = (bf16[1536,256]{1,0:T(8,128)(2,1)S(1)}, bf16[1536,256]{1,0:T(8,128)(2,1)S(1)}, u32[]{:S(2)}, u32[]{:S(2)}) collective-permute-start(bf16[1536,256]{1,0:T(8,128)(2,1)S(1)} %bitcast.7), channel_id=1, source_target_pairs={{0,64},{64,0},{1,65},{65,1},{2,66},{66,2},{3,67},{67,3},{4,68},{68... | collective-permute-start | bytes 2359304 | tf_op jit(solution)/shard_map/ppermute | solution.py:156
  40.1 18.0 %collective-permute-start = (bf16[384,128]{1,0:T(8,128)(2,1)S(1)}, bf16[384,128]{1,0:T(8,128)(2,1)S(1)}, u32[]{:S(2)}, u32[]{:S(2)}) collective-permute-start(bf16[384,128]{1,0:T(8,128)(2,1)S(1)} %slice.10), channel_id=1, source_target_pairs={{0,16},{16,32},{32,48},{48,0},{1,17},{17,33},{33,49},{49,1},{2,18}... | collective-permute-start | bytes 294920 | tf_op jit(solution)/shard_map/ppermute | solution.py:152
  46.1 15.6 %collective-permute-start.1 = (bf16[384,128]{1,0:T(8,128)(2,1)S(1)}, bf16[384,128]{1,0:T(8,128)(2,1)S(1)}, u32[]{:S(2)}, u32[]{:S(2)}) collective-permute-start(bf16[384,128]{1,0:T(8,128)(2,1)S(1)} %slice.10), channel_id=1, source_target_pairs={{0,32},{16,48},{32,0},{48,16},{1,33},{17,49},{33,1},{49,17},{2,34}... | collective-permute-start | bytes 294920 | tf_op jit(solution)/shard_map/ppermute | solution.py:152
  54.4 9.2 %collective-permute-start.2 = (bf16[384,128]{1,0:T(8,128)(2,1)S(1)}, bf16[384,128]{1,0:T(8,128)(2,1)S(1)}, u32[]{:S(2)}, u32[]{:S(2)}) collective-permute-start(bf16[384,128]{1,0:T(8,128)(2,1)S(1)} %slice.10), channel_id=1, source_target_pairs={{0,48},{16,0},{32,16},{48,32},{1,49},{17,1},{33,17},{49,33},{2,50}... | collective-permute-start | bytes 294920 | tf_op jit(solution)/shard_map/ppermute | solution.py:152

commit v2 on v1

v2 whole, which is shorter than its diff:
```python
import functools
import math

import jax
import jax.numpy as jnp
from jax import lax
from jax.experimental import pallas as pl
from jax.experimental.pallas import tpu as pltpu
from jax.sharding import Mesh, PartitionSpec as P

HD = 128
HEADS = 16
TOKENS = 24
SIDE = 8
SCALE = math.log2(math.e) / math.sqrt(HD)
VMEM = pltpu.CompilerParams(vmem_limit_bytes=48 * 1024 * 1024)

AXES = ("yl", "c", "zh", "zl", "x", "yh")
SIZES = (4, 2, 4, 2, 4, 2)
HEAD_GROUP = ("yh", "yl", "zl")
BACK_GROUP = ("zh", "yh", "yl", "zl")


def whole(count):
    return [pl.BlockSpec(memory_space=pltpu.VMEM)] * count


def pack_kernel(q_ref, k_ref, v_ref, out_ref, near_ref, done):
    copies = [
        pltpu.make_async_copy(source, near_ref.at[place], done.at[place])
        for place, source in enumerate((q_ref, k_ref, v_ref))
    ]
    for copy in copies:
        copy.start()
    for place, copy in enumerate(copies):
        copy.wait()
        for head in range(HEADS):
            out_ref[head, :, place * HD : (place + 1) * HD] = near_ref[
                place, :, head * HD : (head + 1) * HD
            ]


def pack(queries, keys, values):
    return pl.pallas_call(
        pack_kernel,
        out_shape=jax.ShapeDtypeStruct((HEADS, TOKENS, 3 * HD), jnp.bfloat16),
        in_specs=[pl.BlockSpec(memory_space=pl.ANY)] * 3,
        out_specs=pl.BlockSpec(memory_space=pltpu.VMEM),
        scratch_shapes=[
            pltpu.VMEM((3, TOKENS, HEADS * HD), jnp.bfloat16),
            pltpu.SemaphoreType.DMA((3,)),
        ],
        name="pack",
    )(queries, keys, values)


def load_keys(kv_ref, keys_ref, wide_ref):
    keys_ref[...] = kv_ref[:, :HD]
    wide_ref[:, :HD] = kv_ref[:, HD:]
    wide_ref[:, HD:] = jnp.ones((kv_ref.shape[0], HD), jnp.bfloat16)


def fold(q_refs, keys_ref, wide_ref, scores_ref, rows, finish):
    each = q_refs[0].shape[0] // rows

    def scores(step):
        return lax.dot_general(
            q_refs[step // each][step % each * rows : (step % each + 1) * rows, :],
            keys_ref[...],
            (((1,), (1,)), ((), ())),
            preferred_element_type=jnp.float32,
        )

    count = len(q_refs) * each
    scores_ref[0] = scores(0)
    for step in range(count):
        if step + 1 < count:
            scores_ref[(step + 1) % 2] = scores(step + 1)
        tile = scores_ref[step % 2]
        top = jnp.max(tile, axis=1, keepdims=True)
        weights = jnp.exp2((tile - top) * SCALE).astype(jnp.bfloat16)
        sums = jnp.dot(weights, wide_ref[...], preferred_element_type=jnp.float32)
        finish(step, top, sums)


def first_kernel(
    q0_ref, q1_ref, q2_ref, q3_ref, kv_ref, top_ref, sums_ref, keys_ref, wide_ref, scores_ref, *, rows
):
    load_keys(kv_ref, keys_ref, wide_ref)

    def finish(step, top, sums):
        span = slice(step * rows, (step + 1) * rows)
        top_ref[span, :] = jnp.broadcast_to(top, (rows, HD))
        sums_ref[span, :] = sums

    fold((q0_ref, q1_ref, q2_ref, q3_ref), keys_ref, wide_ref, scores_ref, rows, finish)


def second_kernel(
    q0_ref,
    q1_ref,
    q2_ref,
    q3_ref,
    kv_ref,
    me_ref,
    top_ref,
    sums_ref,
    out_ref,
    keys_ref,
    wide_ref,
    scores_ref,
    *,
    rows,
):
    load_keys(kv_ref, keys_ref, wide_ref)
    blocks = rows // TOKENS
    each = HEADS // blocks
    lane = lax.broadcasted_iota(jnp.int32, (blocks, SIDE, HD), 2)

    def finish(step, own_top, own_sums):
        span = slice(step * rows, (step + 1) * rows)
        other_top = top_ref[span, :]
        top = jnp.maximum(own_top, other_top)
        own = jnp.exp2((own_top - top) * SCALE)
        other = jnp.exp2((other_top - top) * SCALE)
        total = own_sums[:, HD:] * own + sums_ref[span, HD:] * other
        share = (own_sums[:, :HD] * own + sums_ref[span, :HD] * other) / total
        rest = (jnp.log2(total) + top * SCALE).reshape(blocks, TOKENS, HD)
        side = jnp.zeros((blocks, SIDE, HD), jnp.float32)
        for term in range(3):
            piece = rest.astype(jnp.bfloat16).astype(jnp.float32)
            rest = rest - piece
            for group in range(TOKENS // SIDE):
                side = jnp.where(
                    lane == group * 3 + term, piece[:, group * SIDE : (group + 1) * SIDE, :], side
                )
        source = lax.rem(me_ref[0] + 4 - step // each, 4)
        out_ref[pl.ds(source * HEADS + step % each * blocks, blocks)] = jnp.concatenate(
            [share.reshape(blocks, TOKENS, HD), side], axis=1
        ).astype(jnp.bfloat16)

    fold((q0_ref, q1_ref, q2_ref, q3_ref), keys_ref, wide_ref, scores_ref, rows, finish)


def attend(queries, kv, me, state, rows=192):
    count, keys = 4 * queries[0].shape[0], kv.shape[0]
    specs = whole(5)
    if state is None:
        kernel, operands, name = first_kernel, (*queries, kv), "attend_first"
        out_shape = [
            jax.ShapeDtypeStruct((count, HD), jnp.float32),
            jax.ShapeDtypeStruct((count, 2 * HD), jnp.float32),
        ]
    else:
        kernel, operands, name = second_kernel, (*queries, kv, me, *state), "attend_second"
        specs = specs + [pl.BlockSpec(memory_space=pltpu.SMEM)] + whole(2)
        out_shape = [jax.ShapeDtypeStruct((count // TOKENS, TOKENS + SIDE, HD), jnp.bfloat16)]
    return pl.pallas_call(
        functools.partial(kernel, rows=rows),
        out_shape=out_shape,
        in_specs=specs,
        out_specs=whole(len(out_shape)),
        scratch_shapes=[
            pltpu.VMEM((keys, HD), jnp.bfloat16),
            pltpu.VMEM((keys, 2 * HD), jnp.bfloat16),
            pltpu.VMEM((2, rows, keys), jnp.float32),
        ],
        compiler_params=VMEM,
        cost_estimate=pl.CostEstimate(
            flops=(1 if state else 64) * 8 * count * keys * HD, bytes_accessed=4 << 20, transcendentals=count * keys
        ),
        name=name,
    )(*operands)


def combine_kernel(parts_ref, out_ref):
    for head in range(HEADS):
        blocks = [parts_ref[part * HEADS + head].astype(jnp.float32) for part in range(4)]
        merged = []
        for group in range(TOKENS // SIDE):
            rows = slice(group * SIDE, (group + 1) * SIDE)
            logs = []
            for block in blocks:
                side = block[TOKENS:, group * 3 : group * 3 + 3]
                logs.append(side[:, 0:1] + side[:, 1:2] + side[:, 2:3])
            top = jnp.maximum(jnp.maximum(logs[0], logs[1]), jnp.maximum(logs[2], logs[3]))
            factors = [jnp.exp2(log - top) for log in logs]
            total = (factors[0] + factors[1]) + (factors[2] + factors[3])
            acc = sum(blocks[part][rows] * (factors[part] / total) for part in range(4))
            merged.append(acc)
        out_ref[:, head * HD : (head + 1) * HD] = jnp.concatenate(merged, axis=0).astype(jnp.bfloat16)


def combine(parts):
    return pl.pallas_call(
        combine_kernel,
        out_shape=jax.ShapeDtypeStruct((TOKENS, HEADS * HD), jnp.bfloat16),
        in_specs=whole(1),
        out_specs=pl.BlockSpec(memory_space=pltpu.VMEM),
        compiler_params=VMEM,
        name="combine",
    )(parts)


def spread(array, axis, size):
    copies = jnp.broadcast_to(array[None], (size,) + array.shape)
    gathered = lax.all_to_all(copies, axis, split_axis=0, concat_axis=0, tiled=True)
    return gathered.reshape(size * array.shape[0], array.shape[1])


def per_device(queries, keys, values):
    packed = pack(queries, keys, values)
    mine = lax.all_to_all(packed, HEAD_GROUP, split_axis=0, concat_axis=0, tiled=True)
    mine = mine.reshape(HEADS * TOKENS, 3 * HD)
    own_q = mine[:, :HD]
    kv = spread(mine[:, HD:], "x", 4)
    shifts = [[(source, (source + by) % 4) for source in range(4)] for by in (1, 2, 3)]
    query = [own_q] + [lax.ppermute(own_q, "zh", pairs) for pairs in shifts]
    other_kv = lax.ppermute(kv, "c", [(0, 1), (1, 0)])
    me = lax.axis_index("zh").astype(jnp.int32).reshape(1)
    (parts,) = attend(query, other_kv, me, attend(query, kv, me, None))
    sent = lax.all_to_all(parts, BACK_GROUP, split_axis=0, concat_axis=0, tiled=True)
    return combine(sent)


def solution(mesh):
    fine = Mesh(mesh.devices.reshape(SIZES), AXES)
    placed = P(AXES, None)
    return jax.shard_map(
        per_device, mesh=fine, in_specs=(placed,) * 3, out_specs=placed, check_vma=False
    )
```

time: 99.7 us -> 87.5 us (0.88)
  the two profiles are of different devices: /device:TPU:16 before, /device:TPU:2 now
where the time goes in v2:
time: 87.5 us; the launch traced here: 87 us
  blocking collectives  46.2 us (53%)
  starting transfers between devices  23.5 us (27%)
  Pallas kernels  12.5 us (14%)
  waiting for transfers between devices  3.81 us (4%)
  local copies, waits for them, and re-layouts  0.96 us (1%)
    all_to_all x1, blocking collectives, per_device(): lax.all_to_all(parts, BACK_GROUP, split_axis=0, concat_axis=0, tiled=True)  24.5 us
    all_to_all x1, blocking collectives, per_device(): lax.all_to_all(packed, HEAD_GROUP, split_axis=0, concat_axis=0, tiled=True)  21.7 us
    ppermute x3, starting transfers between devices, per_device(): query = [own_q] + [lax.ppermute(own_q, 'zh', pairs) for pairs in shifts]  16.8 us
    pallas_call x2, Pallas kernels, attend(): pl.pallas_call(functools.partial(kernel, rows=rows), out_shape=out_shape,...  8.78 us
    all_to_all x1, starting transfers between devices, spread(): lax.all_to_all(copies, axis, split_axis=0, concat_axis=0, tiled=True)  4.82 us
    ppermute x3, waiting for transfers between devices, per_device(): query = [own_q] + [lax.ppermute(own_q, 'zh', pairs) for pairs in shifts]  3.81 us
    pallas_call x1, Pallas kernels, combine(): pl.pallas_call(combine_kernel, out_shape=jax.ShapeDtypeStruct((TOKENS, HE...  1.96 us
    ppermute x1, starting transfers between devices, per_device(): other_kv = lax.ppermute(kv, 'c', [(0, 1), (1, 0)])  1.92 us
  transfers between devices with their start and end apart: 5, of which 1 were waited for; matrix products, arithmetic and copies ran while one was open for 0% of the time, Pallas kernels for 5%

profile of v2, /device:TPU:2, one launch (start us, length us, event | category | flops | bytes accessed | tf_op | source)
XLA Modules:
  0.0 87.0 jit_solution(2317414157607422158)
XLA Ops:
  0.0 1.7 %pack.1 = bf16[16,24,384]{2,1,0:T(8,128)(2,1)} custom-call(bf16[24,2048]{1,0:T(8,128)(2,1)} %q_ref.1, bf16[24,2048]{1,0:T(8,128)(2,1)} %k_ref.1, bf16[24,2048]{1,0:T(8,128)(2,1)} %v_ref.1), custom_call_target="tpu_custom_call" | custom-call | tf_op jit(solution)/shard_map/pack/pallas_call | solution.py:44
  1.7 21.7 %all_to_all.15 = bf16[16,24,384]{2,1,0:T(8,128)(2,1)S(1)} all-to-all(bf16[16,24,384]{2,1,0:T(8,128)(2,1)} %pack.1), channel_id=1, replica_groups=mesh['yl'=4,'c'=2,'zh'=4,'zl'=2,'x'=4,'yh'=2] {'yh','yl','zl'}, dimensions={0} | all-to-all | bytes 589824 | tf_op jit(solution)/shard_map/all_to_all | solution.py:213
  23.4 0.9 %broadcast_in_dim.2 = bf16[4,384,256]{2,1,0:T(8,128)(2,1)} broadcast(bf16[384,256]{1,0:T(8,128)(2,1)S(1)} %slice.9), dimensions={1,2} | broadcast | bytes 983040 | tf_op jit(solution)/shard_map/broadcast_in_dim | solution.py:206
  24.4 4.8 %all-to-all-start.1 = ((bf16[4,384,256]{2,1,0:T(8,128)(2,1)}), bf16[4,384,256]{2,1,0:T(8,128)(2,1)}, u32[]{:S(2)}, u32[]{:S(2)}) async-start(bf16[4,384,256]{2,1,0:T(8,128)(2,1)} %broadcast_in_dim.2), calls=%async_computation.1 | async-start | bytes 1572864 | tf_op jit(solution)/shard_map/all_to_all | solution.py:207
  29.2 10.0 %collective-permute-start.2 = (bf16[384,128]{1,0:T(8,128)(2,1)S(1)}, bf16[384,128]{1,0:T(8,128)(2,1)S(1)}, u32[]{:S(2)}, u32[]{:S(2)}) collective-permute-start(bf16[384,128]{1,0:T(8,128)(2,1)S(1)} %slice.8.q0_ref), channel_id=1, source_target_pairs={{0,48},{16,0},{32,16},{48,32},{1,49},{17,1},{33,17},{49,33},{2,50}... | collective-permute-start | bytes 294920 | tf_op jit(solution)/shard_map/ppermute | solution.py:218
  39.2 1.9 %collective-permute-start.1 = (bf16[384,128]{1,0:T(8,128)(2,1)S(1)}, bf16[384,128]{1,0:T(8,128)(2,1)S(1)}, u32[]{:S(2)}, u32[]{:S(2)}) collective-permute-start(bf16[384,128]{1,0:T(8,128)(2,1)S(1)} %slice.8.q0_ref), channel_id=1, source_target_pairs={{0,32},{16,48},{32,0},{48,16},{1,33},{17,49},{33,1},{49,17},{2,34}... | collective-permute-start | bytes 294920 | tf_op jit(solution)/shard_map/ppermute | solution.py:218
  41.2 4.8 %collective-permute-start = (bf16[384,128]{1,0:T(8,128)(2,1)S(1)}, bf16[384,128]{1,0:T(8,128)(2,1)S(1)}, u32[]{:S(2)}, u32[]{:S(2)}) collective-permute-start(bf16[384,128]{1,0:T(8,128)(2,1)S(1)} %slice.8.q0_ref), channel_id=1, source_target_pairs={{0,16},{16,32},{32,48},{48,0},{1,17},{17,33},{33,49},{49,1},{2,18}... | collective-permute-start | bytes 294920 | tf_op jit(solution)/shard_map/ppermute | solution.py:218
  46.0 0.0 all-to-all-done.1
  46.0 1.9 %collective-permute-start.3 = (bf16[1536,256]{1,0:T(8,128)(2,1)}, bf16[1536,256]{1,0:T(8,128)(2,1)}, u32[]{:S(2)}, u32[]{:S(2)}) collective-permute-start(bf16[1536,256]{1,0:T(8,128)(2,1)} %bitcast.1.kv_ref), channel_id=1, source_target_pairs={{0,64},{64,0},{1,65},{65,1},{2,66},{66,2},{3,67},{67,3},{4,68},{68... | collective-permute-start | bytes 2359304 | tf_op jit(solution)/shard_map/ppermute | solution.py:219
  47.9 0.0 collective-permute-done.2.q3_ref
  47.9 3.8 %collective-permute-done.1.q2_ref = bf16[384,128]{1,0:T(8,128)(2,1)S(1)} collective-permute-done((bf16[384,128]{1,0:T(8,128)(2,1)S(1)}, bf16[384,128]{1,0:T(8,128)(2,1)S(1)}, u32[]{:S(2)}, u32[]{:S(2)}) %collective-permute-start.1) | collective-permute-done | bytes 98336 | tf_op jit(solution)/shard_map/ppermute | solution.py:218
  51.7 0.0 collective-permute-done.q1_ref
  51.7 4.3 %attend_first.1 = (f32[1536,128]{1,0:T(8,128)S(1)}, f32[1536,256]{1,0:T(8,128)S(1)}) custom-call(bf16[384,128]{1,0:T(8,128)(2,1)S(1)} %slice.8.q0_ref, bf16[384,128]{1,0:T(8,128)(2,1)S(1)} %collective-permute-done.q1_ref, bf16[384,128]{1,0:T(8,128)(2,1)S(1)} %collective-permute-done.1.q2_ref, bf16[384,128]{1,0:T(8,128)(2,1)S(1)} %collective-permute-done.2.q3_ref, ...), custom_call_target="tpu_custom_call" | custom-call | flops 154618822656 | bytes 4194304 | tf_op jit(solution)/shard_map/attend_first/pallas_call | solution.py:158
  56.1 0.0 collective-permute-done.3.kv_ref
  56.1 4.5 %attend_second.1 = bf16[64,32,128]{2,1,0:T(8,128)(2,1)S(1)} custom-call(bf16[384,128]{1,0:T(8,128)(2,1)S(1)} %slice.8.q0_ref, bf16[384,128]{1,0:T(8,128)(2,1)S(1)} %collective-permute-done.q1_ref, bf16[384,128]{1,0:T(8,128)(2,1)S(1)} %collective-permute-done.1.q2_ref, bf16[384,128]{1,0:T(8,128)(2,1)S(1)} %collective-permute-done.2.q3_ref, ...), custom_call_target="tpu_custom_call" | custom-call | flops 2415919104 | bytes 4194304 | tf_op jit(solution)/shard_map/attend_second/pallas_call | solution.py:158
  60.5 24.5 %all_to_all.16.parts_ref = bf16[64,32,128]{2,1,0:T(8,128)(2,1)S(1)} all-to-all(bf16[64,32,128]{2,1,0:T(8,128)(2,1)S(1)} %attend_second.1), channel_id=1, replica_groups=mesh['yl'=4,'c'=2,'zh'=4,'zl'=2,'x'=4,'yh'=2] {'zh','yh','yl','zl'}, dimensions={0} | all-to-all | bytes 1048576 | tf_op jit(solution)/shard_map/all_to_all | solution.py:222
  85.1 2.0 %combine.1 = bf16[24,2048]{1,0:T(8,128)(2,1)} custom-call(bf16[64,32,128]{2,1,0:T(8,128)(2,1)S(1)} %all_to_all.16.parts_ref), custom_call_target="tpu_custom_call" | custom-call | tf_op jit(solution)/shard_map/combine/pallas_call | solution.py:195
  (2 shorter events, 0.0 us)
Async XLA Ops:
  24.4 21.6 %all-to-all-start.1 = ((bf16[4,384,256]{2,1,0:T(8,128)(2,1)}), bf16[4,384,256]{2,1,0:T(8,128)(2,1)}, u32[]{:S(2)}, u32[]{:S(2)}) async-start(bf16[4,384,256]{2,1,0:T(8,128)(2,1)} %broadcast_in_dim.2), calls=%async_computation.1 | async-start | bytes 1572864 | tf_op jit(solution)/shard_map/all_to_all | solution.py:207
  29.2 18.7 %collective-permute-start.2 = (bf16[384,128]{1,0:T(8,128)(2,1)S(1)}, bf16[384,128]{1,0:T(8,128)(2,1)S(1)}, u32[]{:S(2)}, u32[]{:S(2)}) collective-permute-start(bf16[384,128]{1,0:T(8,128)(2,1)S(1)} %slice.8.q0_ref), channel_id=1, source_target_pairs={{0,48},{16,0},{32,16},{48,32},{1,49},{17,1},{33,17},{49,33},{2,50}... | collective-permute-start | bytes 294920 | tf_op jit(solution)/shard_map/ppermute | solution.py:218
  39.2 12.5 %collective-permute-start.1 = (bf16[384,128]{1,0:T(8,128)(2,1)S(1)}, bf16[384,128]{1,0:T(8,128)(2,1)S(1)}, u32[]{:S(2)}, u32[]{:S(2)}) collective-permute-start(bf16[384,128]{1,0:T(8,128)(2,1)S(1)} %slice.8.q0_ref), channel_id=1, source_target_pairs={{0,32},{16,48},{32,0},{48,16},{1,33},{17,49},{33,1},{49,17},{2,34}... | collective-permute-start | bytes 294920 | tf_op jit(solution)/shard_map/ppermute | solution.py:218
  41.2 10.6 %collective-permute-start = (bf16[384,128]{1,0:T(8,128)(2,1)S(1)}, bf16[384,128]{1,0:T(8,128)(2,1)S(1)}, u32[]{:S(2)}, u32[]{:S(2)}) collective-permute-start(bf16[384,128]{1,0:T(8,128)(2,1)S(1)} %slice.8.q0_ref), channel_id=1, source_target_pairs={{0,16},{16,32},{32,48},{48,0},{1,17},{17,33},{33,49},{49,1},{2,18}... | collective-permute-start | bytes 294920 | tf_op jit(solution)/shard_map/ppermute | solution.py:218
  46.0 10.1 %collective-permute-start.3 = (bf16[1536,256]{1,0:T(8,128)(2,1)}, bf16[1536,256]{1,0:T(8,128)(2,1)}, u32[]{:S(2)}, u32[]{:S(2)}) collective-permute-start(bf16[1536,256]{1,0:T(8,128)(2,1)} %bitcast.1.kv_ref), channel_id=1, source_target_pairs={{0,64},{64,0},{1,65},{65,1},{2,66},{66,2},{3,67},{67,3},{4,68},{68... | collective-permute-start | bytes 2359304 | tf_op jit(solution)/shard_map/ppermute | solution.py:219

commit v3 on v2

--- a/solution.py
+++ b/solution.py
@@ -12,8 +12,9 @@
 HEADS = 16
 TOKENS = 24
 SIDE = 8
+LANES = 9
 SCALE = math.log2(math.e) / math.sqrt(HD)
-VMEM = pltpu.CompilerParams(vmem_limit_bytes=48 * 1024 * 1024)
+VMEM = pltpu.CompilerParams(vmem_limit_bytes=24 * 1024 * 1024)
 
 AXES = ("yl", "c", "zh", "zl", "x", "yh")
 SIZES = (4, 2, 4, 2, 4, 2)
@@ -167,28 +168,38 @@
         ],
         compiler_params=VMEM,
         cost_estimate=pl.CostEstimate(
-            flops=(1 if state else 64) * 8 * count * keys * HD, bytes_accessed=4 << 20, transcendentals=count * keys
+            flops=(1 if state else 4) * 8 * count * keys * HD, bytes_accessed=4 << 20, transcendentals=count * keys
         ),
         name=name,
     )(*operands)
 
 
 def combine_kernel(parts_ref, out_ref):
-    for head in range(HEADS):
-        blocks = [parts_ref[part * HEADS + head].astype(jnp.float32) for part in range(4)]
-        merged = []
-        for group in range(TOKENS // SIDE):
-            rows = slice(group * SIDE, (group + 1) * SIDE)
-            logs = []
-            for block in blocks:
-                side = block[TOKENS:, group * 3 : group * 3 + 3]
-                logs.append(side[:, 0:1] + side[:, 1:2] + side[:, 2:3])
-            top = jnp.maximum(jnp.maximum(logs[0], logs[1]), jnp.maximum(logs[2], logs[3]))
-            factors = [jnp.exp2(log - top) for log in logs]
-            total = (factors[0] + factors[1]) + (factors[2] + factors[3])
-            acc = sum(blocks[part][rows] * (factors[part] / total) for part in range(4))
-            merged.append(acc)
-        out_ref[:, head * HD : (head + 1) * HD] = jnp.concatenate(merged, axis=0).astype(jnp.bfloat16)
+    for first in range(0, HEADS, SIDE):
+        logs = []
+        for part in range(4):
+            side = 0.0
+            for head in range(first, first + SIDE):
+                tile = parts_ref[part * HEADS + head, TOKENS:, :].astype(jnp.float32)
+                if head > first:
+                    tile = pltpu.roll(tile, (head - first) * LANES, 1)
+                side = side + tile
+            logs.append(side + pltpu.roll(side, HD - 1, 1) + pltpu.roll(side, HD - 2, 1))
+        top = jnp.maximum(jnp.maximum(logs[0], logs[1]), jnp.maximum(logs[2], logs[3]))
+        factors = [jnp.exp2(log - top) for log in logs]
+        total = (factors[0] + factors[1]) + (factors[2] + factors[3])
+        factors = [factor / total for factor in factors]
+        for head in range(first, first + SIDE):
+            merged = 0.0
+            for part in range(4):
+                weights = []
+                for group in range(TOKENS // SIDE):
+                    lane = (head - first) * LANES + 3 * group
+                    weight = factors[part][:, lane : lane + 1]
+                    weights.append(jnp.broadcast_to(weight, (SIDE, HD)))
+                rows = parts_ref[part * HEADS + head, :TOKENS, :].astype(jnp.float32)
+                merged = merged + rows * jnp.concatenate(weights, axis=0)
+            out_ref[:, head * HD : (head + 1) * HD] = merged.astype(jnp.bfloat16)
 
 
 def combine(parts):

time: 87.5 us -> 84.6 us (0.967)
  Pallas kernels: 12.5 us -> 9.6 us
    pallas_call x2, Pallas kernels: 8.78 us -> 6.51 us  [attend(): pl.pallas_call(functools.partial(kernel, rows=rows), out_shape=out_shape,...]
  transfers between devices with their start and end apart: 5 -> 5, of which waited for: 1 -> 2; matrix products, arithmetic and copies ran while one was open for 0% -> 0% of each run, Pallas kernels for 5% -> 4%
where the time goes in v3:
time: 84.6 us; the launch traced here: 84.1 us
  blocking collectives  46.2 us (55%)
  starting transfers between devices  23.5 us (28%)
  Pallas kernels  9.6 us (11%)
  waiting for transfers between devices  3.78 us (4%)
  local copies, waits for them, and re-layouts  0.97 us (1%)
    all_to_all x1, blocking collectives, per_device(): lax.all_to_all(parts, BACK_GROUP, split_axis=0, concat_axis=0, tiled=True)  24.5 us
    all_to_all x1, blocking collectives, per_device(): lax.all_to_all(packed, HEAD_GROUP, split_axis=0, concat_axis=0, tiled=True)  21.7 us
    ppermute x3, starting transfers between devices, per_device(): query = [own_q] + [lax.ppermute(own_q, 'zh', pairs) for pairs in shifts]  16.8 us
    pallas_call x2, Pallas kernels, attend(): pl.pallas_call(functools.partial(kernel, rows=rows), out_shape=out_shape,...  6.51 us
    all_to_all x1, starting transfers between devices, spread(): lax.all_to_all(copies, axis, split_axis=0, concat_axis=0, tiled=True)  4.82 us
    ppermute x3, waiting for transfers between devices, per_device(): query = [own_q] + [lax.ppermute(own_q, 'zh', pairs) for pairs in shifts]  3.78 us
    ppermute x1, starting transfers between devices, per_device(): other_kv = lax.ppermute(kv, 'c', [(0, 1), (1, 0)])  1.92 us
    pallas_call x1, Pallas kernels, pack(): pl.pallas_call(pack_kernel, out_shape=jax.ShapeDtypeStruct((HEADS, TOKENS...  1.73 us
  transfers between devices with their start and end apart: 5, of which 2 were waited for; matrix products, arithmetic and copies ran while one was open for 0% of the time, Pallas kernels for 4%

profile of v3, /device:TPU:2, one launch (start us, length us, event | category | flops | bytes accessed | tf_op | source)
XLA Modules:
  0.0 84.1 jit_solution(5253441286464429581)
XLA Ops:
  0.0 1.7 %pack.1 = bf16[16,24,384]{2,1,0:T(8,128)(2,1)} custom-call(bf16[24,2048]{1,0:T(8,128)(2,1)} %q_ref.1, bf16[24,2048]{1,0:T(8,128)(2,1)} %k_ref.1, bf16[24,2048]{1,0:T(8,128)(2,1)} %v_ref.1), custom_call_target="tpu_custom_call" | custom-call | tf_op jit(solution)/shard_map/pack/pallas_call | solution.py:45
  1.7 21.7 %all_to_all.15 = bf16[16,24,384]{2,1,0:T(8,128)(2,1)S(1)} all-to-all(bf16[16,24,384]{2,1,0:T(8,128)(2,1)} %pack.1), channel_id=1, replica_groups=mesh['yl'=4,'c'=2,'zh'=4,'zl'=2,'x'=4,'yh'=2] {'yh','yl','zl'}, dimensions={0} | all-to-all | bytes 589824 | tf_op jit(solution)/shard_map/all_to_all | solution.py:224
  23.4 0.9 %broadcast_in_dim.2 = bf16[4,384,256]{2,1,0:T(8,128)(2,1)} broadcast(bf16[384,256]{1,0:T(8,128)(2,1)S(1)} %slice.9), dimensions={1,2} | broadcast | bytes 983040 | tf_op jit(solution)/shard_map/broadcast_in_dim | solution.py:217
  24.4 4.8 %all-to-all-start.1 = ((bf16[4,384,256]{2,1,0:T(8,128)(2,1)}), bf16[4,384,256]{2,1,0:T(8,128)(2,1)S(1)}, u32[]{:S(2)}, u32[]{:S(2)}) async-start(bf16[4,384,256]{2,1,0:T(8,128)(2,1)} %broadcast_in_dim.2), calls=%async_computation.1 | async-start | bytes 1572864 | tf_op jit(solution)/shard_map/all_to_all | solution.py:218
  29.2 10.0 %collective-permute-start.2 = (bf16[384,128]{1,0:T(8,128)(2,1)S(1)}, bf16[384,128]{1,0:T(8,128)(2,1)S(1)}, u32[]{:S(2)}, u32[]{:S(2)}) collective-permute-start(bf16[384,128]{1,0:T(8,128)(2,1)S(1)} %slice.8.q0_ref), channel_id=1, source_target_pairs={{0,48},{16,0},{32,16},{48,32},{1,49},{17,1},{33,17},{49,33},{2,50}... | collective-permute-start | bytes 294920 | tf_op jit(solution)/shard_map/ppermute | solution.py:229
  39.3 1.9 %collective-permute-start.1 = (bf16[384,128]{1,0:T(8,128)(2,1)S(1)}, bf16[384,128]{1,0:T(8,128)(2,1)S(1)}, u32[]{:S(2)}, u32[]{:S(2)}) collective-permute-start(bf16[384,128]{1,0:T(8,128)(2,1)S(1)} %slice.8.q0_ref), channel_id=1, source_target_pairs={{0,32},{16,48},{32,0},{48,16},{1,33},{17,49},{33,1},{49,17},{2,34}... | collective-permute-start | bytes 294920 | tf_op jit(solution)/shard_map/ppermute | solution.py:229
  41.2 4.8 %collective-permute-start = (bf16[384,128]{1,0:T(8,128)(2,1)S(1)}, bf16[384,128]{1,0:T(8,128)(2,1)S(1)}, u32[]{:S(2)}, u32[]{:S(2)}) collective-permute-start(bf16[384,128]{1,0:T(8,128)(2,1)S(1)} %slice.8.q0_ref), channel_id=1, source_target_pairs={{0,16},{16,32},{32,48},{48,0},{1,17},{17,33},{33,49},{49,1},{2,18}... | collective-permute-start | bytes 294920 | tf_op jit(solution)/shard_map/ppermute | solution.py:229
  46.0 0.0 all-to-all-done.1
  46.0 1.9 %collective-permute-start.3 = (bf16[1536,256]{1,0:T(8,128)(2,1)S(1)}, bf16[1536,256]{1,0:T(8,128)(2,1)S(1)}, u32[]{:S(2)}, u32[]{:S(2)}) collective-permute-start(bf16[1536,256]{1,0:T(8,128)(2,1)S(1)} %bitcast.3), channel_id=1, source_target_pairs={{0,64},{64,0},{1,65},{65,1},{2,66},{66,2},{3,67},{67,3},{4,68},{68... | collective-permute-start | bytes 2359304 | tf_op jit(solution)/shard_map/ppermute | solution.py:230
  47.9 0.0 collective-permute-done.2.q3_ref
  47.9 3.6 %collective-permute-done.1.q2_ref = bf16[384,128]{1,0:T(8,128)(2,1)S(1)} collective-permute-done((bf16[384,128]{1,0:T(8,128)(2,1)S(1)}, bf16[384,128]{1,0:T(8,128)(2,1)S(1)}, u32[]{:S(2)}, u32[]{:S(2)}) %collective-permute-start.1) | collective-permute-done | bytes 98336 | tf_op jit(solution)/shard_map/ppermute | solution.py:229
  51.6 0.1 collective-permute-done.q1_ref
  51.7 3.2 %attend_first.1 = (f32[1536,128]{1,0:T(8,128)S(1)}, f32[1536,256]{1,0:T(8,128)S(1)}) custom-call(bf16[384,128]{1,0:T(8,128)(2,1)S(1)} %slice.8.q0_ref, bf16[384,128]{1,0:T(8,128)(2,1)S(1)} %collective-permute-done.q1_ref, bf16[384,128]{1,0:T(8,128)(2,1)S(1)} %collective-permute-done.1.q2_ref, bf16[384,128]{1,0:T(8,128)(2,1)S(1)} %collective-permute-done.2.q3_ref, ...), custom_call_target="tpu_custom_call" | custom-call | flops 9663676416 | bytes 4194304 | tf_op jit(solution)/shard_map/attend_first/pallas_call | solution.py:159
  54.9 0.0 collective-permute-done.3.kv_ref
  54.9 3.3 %attend_second.1 = bf16[64,32,128]{2,1,0:T(8,128)(2,1)S(1)} custom-call(bf16[384,128]{1,0:T(8,128)(2,1)S(1)} %slice.8.q0_ref, bf16[384,128]{1,0:T(8,128)(2,1)S(1)} %collective-permute-done.q1_ref, bf16[384,128]{1,0:T(8,128)(2,1)S(1)} %collective-permute-done.1.q2_ref, bf16[384,128]{1,0:T(8,128)(2,1)S(1)} %collective-permute-done.2.q3_ref, ...), custom_call_target="tpu_custom_call" | custom-call | flops 2415919104 | bytes 4194304 | tf_op jit(solution)/shard_map/attend_second/pallas_call | solution.py:159
  58.3 24.5 %all_to_all.16.parts_ref = bf16[64,32,128]{2,1,0:T(8,128)(2,1)S(1)} all-to-all(bf16[64,32,128]{2,1,0:T(8,128)(2,1)S(1)} %attend_second.1), channel_id=1, replica_groups=mesh['yl'=4,'c'=2,'zh'=4,'zl'=2,'x'=4,'yh'=2] {'zh','yh','yl','zl'}, dimensions={0} | all-to-all | bytes 1048576 | tf_op jit(solution)/shard_map/all_to_all | solution.py:233
  82.8 1.4 %combine.1 = bf16[24,2048]{1,0:T(8,128)(2,1)} custom-call(bf16[64,32,128]{2,1,0:T(8,128)(2,1)S(1)} %all_to_all.16.parts_ref), custom_call_target="tpu_custom_call" | custom-call | tf_op jit(solution)/shard_map/combine/pallas_call | solution.py:206
  (2 shorter events, 0.0 us)
Async XLA Ops:
  24.4 21.6 %all-to-all-start.1 = ((bf16[4,384,256]{2,1,0:T(8,128)(2,1)}), bf16[4,384,256]{2,1,0:T(8,128)(2,1)S(1)}, u32[]{:S(2)}, u32[]{:S(2)}) async-start(bf16[4,384,256]{2,1,0:T(8,128)(2,1)} %broadcast_in_dim.2), calls=%async_computation.1 | async-start | bytes 1572864 | tf_op jit(solution)/shard_map/all_to_all | solution.py:218
  29.2 18.7 %collective-permute-start.2 = (bf16[384,128]{1,0:T(8,128)(2,1)S(1)}, bf16[384,128]{1,0:T(8,128)(2,1)S(1)}, u32[]{:S(2)}, u32[]{:S(2)}) collective-permute-start(bf16[384,128]{1,0:T(8,128)(2,1)S(1)} %slice.8.q0_ref), channel_id=1, source_target_pairs={{0,48},{16,0},{32,16},{48,32},{1,49},{17,1},{33,17},{49,33},{2,50}... | collective-permute-start | bytes 294920 | tf_op jit(solution)/shard_map/ppermute | solution.py:229
  39.3 12.3 %collective-permute-start.1 = (bf16[384,128]{1,0:T(8,128)(2,1)S(1)}, bf16[384,128]{1,0:T(8,128)(2,1)S(1)}, u32[]{:S(2)}, u32[]{:S(2)}) collective-permute-start(bf16[384,128]{1,0:T(8,128)(2,1)S(1)} %slice.8.q0_ref), channel_id=1, source_target_pairs={{0,32},{16,48},{32,0},{48,16},{1,33},{17,49},{33,1},{49,17},{2,34}... | collective-permute-start | bytes 294920 | tf_op jit(solution)/shard_map/ppermute | solution.py:229
  41.2 10.5 %collective-permute-start = (bf16[384,128]{1,0:T(8,128)(2,1)S(1)}, bf16[384,128]{1,0:T(8,128)(2,1)S(1)}, u32[]{:S(2)}, u32[]{:S(2)}) collective-permute-start(bf16[384,128]{1,0:T(8,128)(2,1)S(1)} %slice.8.q0_ref), channel_id=1, source_target_pairs={{0,16},{16,32},{32,48},{48,0},{1,17},{17,33},{33,49},{49,1},{2,18}... | collective-permute-start | bytes 294920 | tf_op jit(solution)/shard_map/ppermute | solution.py:229
  46.0 8.9 %collective-permute-start.3 = (bf16[1536,256]{1,0:T(8,128)(2,1)S(1)}, bf16[1536,256]{1,0:T(8,128)(2,1)S(1)}, u32[]{:S(2)}, u32[]{:S(2)}) collective-permute-start(bf16[1536,256]{1,0:T(8,128)(2,1)S(1)} %bitcast.3), channel_id=1, source_target_pairs={{0,64},{64,0},{1,65},{65,1},{2,66},{66,2},{3,67},{67,3},{4,68},{68... | collective-permute-start | bytes 2359304 | tf_op jit(solution)/shard_map/ppermute | solution.py:230

commit v4 on v3

--- a/solution.py
+++ b/solution.py
@@ -13,6 +13,8 @@
 TOKENS = 24
 SIDE = 8
 LANES = 9
+TURNS = (0, 1, 3, 2)
+FIRST = 64
 SCALE = math.log2(math.e) / math.sqrt(HD)
 VMEM = pltpu.CompilerParams(vmem_limit_bytes=24 * 1024 * 1024)
 
@@ -84,17 +86,21 @@
         finish(step, top, sums)
 
 
-def first_kernel(
-    q0_ref, q1_ref, q2_ref, q3_ref, kv_ref, top_ref, sums_ref, keys_ref, wide_ref, scores_ref, *, rows
-):
-    load_keys(kv_ref, keys_ref, wide_ref)
-
+def store_state(top_ref, sums_ref, rows):
     def finish(step, top, sums):
         span = slice(step * rows, (step + 1) * rows)
         top_ref[span, :] = jnp.broadcast_to(top, (rows, HD))
         sums_ref[span, :] = sums
 
-    fold((q0_ref, q1_ref, q2_ref, q3_ref), keys_ref, wide_ref, scores_ref, rows, finish)
+    return finish
+
+
+def first_kernel(
+    q0_ref, q1_ref, q2_ref, kv_ref, top_ref, sums_ref, keys_ref, wide_ref, scores_ref, *, rows
+):
+    load_keys(kv_ref, keys_ref, wide_ref)
+    q_refs = (q0_ref, q1_ref, q2_ref)
+    fold(q_refs, keys_ref, wide_ref, scores_ref, rows, store_state(top_ref, sums_ref, rows))
 
 
 def second_kernel(
@@ -103,6 +109,7 @@
     q2_ref,
     q3_ref,
     kv_ref,
+    other_ref,
     me_ref,
     top_ref,
     sums_ref,
@@ -110,22 +117,31 @@
     keys_ref,
     wide_ref,
     scores_ref,
+    other_keys_ref,
+    other_wide_ref,
+    last_top_ref,
+    last_sums_ref,
     *,
     rows,
 ):
     load_keys(kv_ref, keys_ref, wide_ref)
+    load_keys(other_ref, other_keys_ref, other_wide_ref)
+    last = store_state(last_top_ref, last_sums_ref, rows)
+    fold((q3_ref,), keys_ref, wide_ref, scores_ref, rows, last)
     blocks = rows // TOKENS
     each = HEADS // blocks
     lane = lax.broadcasted_iota(jnp.int32, (blocks, SIDE, HD), 2)
 
     def finish(step, own_top, own_sums):
-        span = slice(step * rows, (step + 1) * rows)
-        other_top = top_ref[span, :]
-        top = jnp.maximum(own_top, other_top)
+        done = step if step < 3 * each else step - 3 * each
+        span = slice(done * rows, (done + 1) * rows)
+        before_top = (top_ref if step < 3 * each else last_top_ref)[span, :]
+        before_sums = (sums_ref if step < 3 * each else last_sums_ref)[span, :]
+        top = jnp.maximum(own_top, before_top)
         own = jnp.exp2((own_top - top) * SCALE)
-        other = jnp.exp2((other_top - top) * SCALE)
-        total = own_sums[:, HD:] * own + sums_ref[span, HD:] * other
-        share = (own_sums[:, :HD] * own + sums_ref[span, :HD] * other) / total
+        before = jnp.exp2((before_top - top) * SCALE)
+        total = own_sums[:, HD:] * own + before_sums[:, HD:] * before
+        share = (own_sums[:, :HD] * own + before_sums[:, :HD] * before) / total
         rest = (jnp.log2(total) + top * SCALE).reshape(blocks, TOKENS, HD)
         side = jnp.zeros((blocks, SIDE, HD), jnp.float32)
         for term in range(3):
@@ -135,43 +151,51 @@
                 side = jnp.where(
                     lane == group * 3 + term, piece[:, group * SIDE : (group + 1) * SIDE, :], side
                 )
-        source = lax.rem(me_ref[0] + 4 - step // each, 4)
+        source = me_ref[0] ^ TURNS[step // each]
         out_ref[pl.ds(source * HEADS + step % each * blocks, blocks)] = jnp.concatenate(
             [share.reshape(blocks, TOKENS, HD), side], axis=1
         ).astype(jnp.bfloat16)
 
-    fold((q0_ref, q1_ref, q2_ref, q3_ref), keys_ref, wide_ref, scores_ref, rows, finish)
-
-
-def attend(queries, kv, me, state, rows=192):
-    count, keys = 4 * queries[0].shape[0], kv.shape[0]
-    specs = whole(5)
-    if state is None:
-        kernel, operands, name = first_kernel, (*queries, kv), "attend_first"
-        out_shape = [
-            jax.ShapeDtypeStruct((count, HD), jnp.float32),
-            jax.ShapeDtypeStruct((count, 2 * HD), jnp.float32),
-        ]
-    else:
-        kernel, operands, name = second_kernel, (*queries, kv, me, *state), "attend_second"
-        specs = specs + [pl.BlockSpec(memory_space=pltpu.SMEM)] + whole(2)
-        out_shape = [jax.ShapeDtypeStruct((count // TOKENS, TOKENS + SIDE, HD), jnp.bfloat16)]
-    return pl.pallas_call(
-        functools.partial(kernel, rows=rows),
-        out_shape=out_shape,
-        in_specs=specs,
-        out_specs=whole(len(out_shape)),
-        scratch_shapes=[
-            pltpu.VMEM((keys, HD), jnp.bfloat16),
-            pltpu.VMEM((keys, 2 * HD), jnp.bfloat16),
-            pltpu.VMEM((2, rows, keys), jnp.float32),
+    q_refs = (q0_ref, q1_ref, q2_ref, q3_ref)
+    fold(q_refs, other_keys_ref, other_wide_ref, scores_ref, rows, finish)
+
+
+def attend(queries, kv, other_kv, me, rows=192):
+    slot, keys = queries[0].shape[0], kv.shape[0]
+    scratch = [
+        pltpu.VMEM((keys, HD), jnp.bfloat16),
+        pltpu.VMEM((keys, 2 * HD), jnp.bfloat16),
+        pltpu.VMEM((2, rows, keys), jnp.float32),
+    ]
+    state = pl.pallas_call(
+        functools.partial(first_kernel, rows=rows),
+        out_shape=[
+            jax.ShapeDtypeStruct((3 * slot, HD), jnp.float32),
+            jax.ShapeDtypeStruct((3 * slot, 2 * HD), jnp.float32),
         ],
+        in_specs=whole(4),
+        out_specs=whole(2),
+        scratch_shapes=scratch,
         compiler_params=VMEM,
         cost_estimate=pl.CostEstimate(
-            flops=(1 if state else 4) * 8 * count * keys * HD, bytes_accessed=4 << 20, transcendentals=count * keys
+            flops=FIRST * 3 * slot * keys * HD, bytes_accessed=4 << 20, transcendentals=3 * slot * keys
         ),
-        name=name,
-    )(*operands)
+        name="attend_first",
+    )(*queries[:3], kv)
+    return pl.pallas_call(
+        functools.partial(second_kernel, rows=rows),
+        out_shape=jax.ShapeDtypeStruct((4 * slot // TOKENS, TOKENS + SIDE, HD), jnp.bfloat16),
+        in_specs=whole(6) + [pl.BlockSpec(memory_space=pltpu.SMEM)] + whole(2),
+        out_specs=pl.BlockSpec(memory_space=pltpu.VMEM),
+        scratch_shapes=scratch
+        + scratch[:2]
+        + [pltpu.VMEM((slot, HD), jnp.float32), pltpu.VMEM((slot, 2 * HD), jnp.float32)],
+        compiler_params=VMEM,
+        cost_estimate=pl.CostEstimate(
+            flops=8 * 5 * slot * keys * HD, bytes_accessed=4 << 20, transcendentals=5 * slot * keys
+        ),
+        name="attend_second",
+    )(*queries, kv, other_kv, me, *state)
 
 
 def combine_kernel(parts_ref, out_ref):
@@ -219,17 +243,20 @@
     return gathered.reshape(size * array.shape[0], array.shape[1])
 
 
+def swap(by):
+    return [(source, source ^ by) for source in range(4)]
+
+
 def per_device(queries, keys, values):
     packed = pack(queries, keys, values)
     mine = lax.all_to_all(packed, HEAD_GROUP, split_axis=0, concat_axis=0, tiled=True)
     mine = mine.reshape(HEADS * TOKENS, 3 * HD)
     own_q = mine[:, :HD]
     kv = spread(mine[:, HD:], "x", 4)
-    shifts = [[(source, (source + by) % 4) for source in range(4)] for by in (1, 2, 3)]
-    query = [own_q] + [lax.ppermute(own_q, "zh", pairs) for pairs in shifts]
+    query = [own_q] + [lax.ppermute(own_q, "zh", swap(by)) for by in TURNS[1:]]
     other_kv = lax.ppermute(kv, "c", [(0, 1), (1, 0)])
     me = lax.axis_index("zh").astype(jnp.int32).reshape(1)
-    (parts,) = attend(query, other_kv, me, attend(query, kv, me, None))
+    parts = attend(query, kv, other_kv, me)
     sent = lax.all_to_all(parts, BACK_GROUP, split_axis=0, concat_axis=0, tiled=True)
     return combine(sent)
 

time: 84.6 us -> 82 us (0.969)
  blocking collectives: 46.2 us -> 44.7 us
    all_to_all x1, blocking collectives: 24.5 us -> 23 us  [per_device(): lax.all_to_all(parts, BACK_GROUP, split_axis=0, concat_axis=0, tiled=True)]
  transfers between devices with their start and end apart: 5 -> 5, of which waited for: 2 -> 2; matrix products, arithmetic and copies ran while one was open for 0% -> 0% of each run, Pallas kernels for 4% -> 3%
where the time goes in v4:
time: 82 us; the launch traced here: 81.6 us
  blocking collectives  44.7 us (55%)
  starting transfers between devices  23 us (28%)
  Pallas kernels  9.84 us (12%)
  waiting for transfers between devices  3.02 us (4%)
  local copies, waits for them, and re-layouts  0.97 us (1%)
    all_to_all x1, blocking collectives, per_device(): lax.all_to_all(parts, BACK_GROUP, split_axis=0, concat_axis=0, tiled=True)  23 us
    all_to_all x1, blocking collectives, per_device(): lax.all_to_all(packed, HEAD_GROUP, split_axis=0, concat_axis=0, tiled=True)  21.7 us
    ppermute x3, starting transfers between devices, per_device(): query = [own_q] + [lax.ppermute(own_q, 'zh', swap(by)) for by in TURNS[1:]]  16.2 us
    all_to_all x1, starting transfers between devices, spread(): lax.all_to_all(copies, axis, split_axis=0, concat_axis=0, tiled=True)  4.82 us
    pallas_call x1, Pallas kernels, attend(): pl.pallas_call(functools.partial(second_kernel, rows=rows), out_shape=jax...  4.25 us
    ppermute x3, waiting for transfers between devices, per_device(): query = [own_q] + [lax.ppermute(own_q, 'zh', swap(by)) for by in TURNS[1:]]  3.02 us
    pallas_call x1, Pallas kernels, attend(): pl.pallas_call(functools.partial(first_kernel, rows=rows), out_shape=[jax...  2.5 us
    ppermute x1, starting transfers between devices, per_device(): other_kv = lax.ppermute(kv, 'c', [(0, 1), (1, 0)])  1.92 us
  transfers between devices with their start and end apart: 5, of which 2 were waited for; matrix products, arithmetic and copies ran while one was open for 0% of the time, Pallas kernels for 3%

profile of v4, /device:TPU:2, one launch (start us, length us, event | category | flops | bytes accessed | tf_op | source)
XLA Modules:
  0.0 81.6 jit_solution(1342589016752040319)
XLA Ops:
  0.0 1.7 %pack.1 = bf16[16,24,384]{2,1,0:T(8,128)(2,1)} custom-call(bf16[24,2048]{1,0:T(8,128)(2,1)} %q_ref.1, bf16[24,2048]{1,0:T(8,128)(2,1)} %k_ref.1, bf16[24,2048]{1,0:T(8,128)(2,1)} %v_ref.1), custom_call_target="tpu_custom_call" | custom-call | tf_op jit(solution)/shard_map/pack/pallas_call | solution.py:47
  1.7 21.7 %all_to_all.15 = bf16[16,24,384]{2,1,0:T(8,128)(2,1)S(1)} all-to-all(bf16[16,24,384]{2,1,0:T(8,128)(2,1)} %pack.1), channel_id=1, replica_groups=mesh['yl'=4,'c'=2,'zh'=4,'zl'=2,'x'=4,'yh'=2] {'yh','yl','zl'}, dimensions={0} | all-to-all | bytes 589824 | tf_op jit(solution)/shard_map/all_to_all | solution.py:252
  23.4 0.9 %broadcast_in_dim.2 = bf16[4,384,256]{2,1,0:T(8,128)(2,1)} broadcast(bf16[384,256]{1,0:T(8,128)(2,1)S(1)} %slice.9), dimensions={1,2} | broadcast | bytes 983040 | tf_op jit(solution)/shard_map/broadcast_in_dim | solution.py:241
  24.4 4.8 %all-to-all-start.1 = ((bf16[4,384,256]{2,1,0:T(8,128)(2,1)}), bf16[4,384,256]{2,1,0:T(8,128)(2,1)S(1)}, u32[]{:S(2)}, u32[]{:S(2)}) async-start(bf16[4,384,256]{2,1,0:T(8,128)(2,1)} %broadcast_in_dim.2), calls=%async_computation.1 | async-start | bytes 1572864 | tf_op jit(solution)/shard_map/all_to_all | solution.py:242
  29.2 10.0 %collective-permute-start.1 = (bf16[384,128]{1,0:T(8,128)(2,1)S(1)}, bf16[384,128]{1,0:T(8,128)(2,1)S(1)}, u32[]{:S(2)}, u32[]{:S(2)}) collective-permute-start(bf16[384,128]{1,0:T(8,128)(2,1)S(1)} %slice.8.q0_ref), channel_id=1, source_target_pairs={{0,48},{16,32},{32,16},{48,0},{1,49},{17,33},{33,17},{49,1},{2,50}... | collective-permute-start | bytes 294920 | tf_op jit(solution)/shard_map/ppermute | solution.py:256
  39.3 2.5 %collective-permute-start = (bf16[384,128]{1,0:T(8,128)(2,1)S(1)}, bf16[384,128]{1,0:T(8,128)(2,1)S(1)}, u32[]{:S(2)}, u32[]{:S(2)}) collective-permute-start(bf16[384,128]{1,0:T(8,128)(2,1)S(1)} %slice.8.q0_ref), channel_id=1, source_target_pairs={{0,16},{16,0},{32,48},{48,32},{1,17},{17,1},{33,49},{49,33},{2,18}... | collective-permute-start | bytes 294920 | tf_op jit(solution)/shard_map/ppermute | solution.py:256
  41.7 3.7 %collective-permute-start.2 = (bf16[384,128]{1,0:T(8,128)(2,1)S(1)}, bf16[384,128]{1,0:T(8,128)(2,1)S(1)}, u32[]{:S(2)}, u32[]{:S(2)}) collective-permute-start(bf16[384,128]{1,0:T(8,128)(2,1)S(1)} %slice.8.q0_ref), channel_id=1, source_target_pairs={{0,32},{16,48},{32,0},{48,16},{1,33},{17,49},{33,1},{49,17},{2,34}... | collective-permute-start | bytes 294920 | tf_op jit(solution)/shard_map/ppermute | solution.py:256
  45.5 0.0 all-to-all-done.1
  45.5 1.9 %collective-permute-start.3 = (bf16[1536,256]{1,0:T(8,128)(2,1)S(1)}, bf16[1536,256]{1,0:T(8,128)(2,1)S(1)}, u32[]{:S(2)}, u32[]{:S(2)}) collective-permute-start(bf16[1536,256]{1,0:T(8,128)(2,1)S(1)} %bitcast.3), channel_id=1, source_target_pairs={{0,64},{64,0},{1,65},{65,1},{2,66},{66,2},{3,67},{67,3},{4,68},{68... | collective-permute-start | bytes 2359304 | tf_op jit(solution)/shard_map/ppermute | solution.py:257
  47.4 0.0 collective-permute-done.1.q2_ref
  47.4 2.4 %collective-permute-done.q1_ref = bf16[384,128]{1,0:T(8,128)(2,1)S(1)} collective-permute-done((bf16[384,128]{1,0:T(8,128)(2,1)S(1)}, bf16[384,128]{1,0:T(8,128)(2,1)S(1)}, u32[]{:S(2)}, u32[]{:S(2)}) %collective-permute-start) | collective-permute-done | bytes 98336 | tf_op jit(solution)/shard_map/ppermute | solution.py:256
  49.8 2.5 %attend_first.1 = (f32[1152,128]{1,0:T(8,128)S(1)}, f32[1152,256]{1,0:T(8,128)S(1)}) custom-call(bf16[384,128]{1,0:T(8,128)(2,1)S(1)} %slice.8.q0_ref, bf16[384,128]{1,0:T(8,128)(2,1)S(1)} %collective-permute-done.q1_ref, bf16[384,128]{1,0:T(8,128)(2,1)S(1)} %collective-permute-done.1.q2_ref, bf16[1536,256]{1,0:T(8,128)(2,1)S(1)} %bitcast.4), custom_call_target="tpu_custom_call" | custom-call | flops 14495514624 | bytes 4194304 | tf_op jit(solution)/shard_map/attend_first/pallas_call | solution.py:170
  52.4 0.6 collective-permute-done.2.q3_ref
  52.9 0.0 collective-permute-done.3.other_ref
  52.9 4.3 %attend_second.1 = bf16[64,32,128]{2,1,0:T(8,128)(2,1)S(1)} custom-call(bf16[384,128]{1,0:T(8,128)(2,1)S(1)} %slice.8.q0_ref, bf16[384,128]{1,0:T(8,128)(2,1)S(1)} %collective-permute-done.q1_ref, bf16[384,128]{1,0:T(8,128)(2,1)S(1)} %collective-permute-done.1.q2_ref, bf16[384,128]{1,0:T(8,128)(2,1)S(1)} %collective-permute-done.2.q3_ref, ...), custom_call_target="tpu_custom_call" | custom-call | flops 3019898880 | bytes 4194304 | tf_op jit(solution)/shard_map/attend_second/pallas_call | solution.py:185
  57.2 23.0 %all_to_all.16.parts_ref = bf16[64,32,128]{2,1,0:T(8,128)(2,1)S(1)} all-to-all(bf16[64,32,128]{2,1,0:T(8,128)(2,1)S(1)} %attend_second.1), channel_id=1, replica_groups=mesh['yl'=4,'c'=2,'zh'=4,'zl'=2,'x'=4,'yh'=2] {'zh','yh','yl','zl'}, dimensions={0} | all-to-all | bytes 1048576 | tf_op jit(solution)/shard_map/all_to_all | solution.py:260
  80.2 1.4 %combine.1 = bf16[24,2048]{1,0:T(8,128)(2,1)} custom-call(bf16[64,32,128]{2,1,0:T(8,128)(2,1)S(1)} %all_to_all.16.parts_ref), custom_call_target="tpu_custom_call" | custom-call | tf_op jit(solution)/shard_map/combine/pallas_call | solution.py:230
  (2 shorter events, 0.0 us)
Async XLA Ops:
  24.4 21.1 %all-to-all-start.1 = ((bf16[4,384,256]{2,1,0:T(8,128)(2,1)}), bf16[4,384,256]{2,1,0:T(8,128)(2,1)S(1)}, u32[]{:S(2)}, u32[]{:S(2)}) async-start(bf16[4,384,256]{2,1,0:T(8,128)(2,1)} %broadcast_in_dim.2), calls=%async_computation.1 | async-start | bytes 1572864 | tf_op jit(solution)/shard_map/all_to_all | solution.py:242
  29.2 18.2 %collective-permute-start.1 = (bf16[384,128]{1,0:T(8,128)(2,1)S(1)}, bf16[384,128]{1,0:T(8,128)(2,1)S(1)}, u32[]{:S(2)}, u32[]{:S(2)}) collective-permute-start(bf16[384,128]{1,0:T(8,128)(2,1)S(1)} %slice.8.q0_ref), channel_id=1, source_target_pairs={{0,48},{16,32},{32,16},{48,0},{1,49},{17,33},{33,17},{49,1},{2,50}... | collective-permute-start | bytes 294920 | tf_op jit(solution)/shard_map/ppermute | solution.py:256
  39.3 10.6 %collective-permute-start = (bf16[384,128]{1,0:T(8,128)(2,1)S(1)}, bf16[384,128]{1,0:T(8,128)(2,1)S(1)}, u32[]{:S(2)}, u32[]{:S(2)}) collective-permute-start(bf16[384,128]{1,0:T(8,128)(2,1)S(1)} %slice.8.q0_ref), channel_id=1, source_target_pairs={{0,16},{16,0},{32,48},{48,32},{1,17},{17,1},{33,49},{49,33},{2,18}... | collective-permute-start | bytes 294920 | tf_op jit(solution)/shard_map/ppermute | solution.py:256
  41.7 11.2 %collective-permute-start.2 = (bf16[384,128]{1,0:T(8,128)(2,1)S(1)}, bf16[384,128]{1,0:T(8,128)(2,1)S(1)}, u32[]{:S(2)}, u32[]{:S(2)}) collective-permute-start(bf16[384,128]{1,0:T(8,128)(2,1)S(1)} %slice.8.q0_ref), channel_id=1, source_target_pairs={{0,32},{16,48},{32,0},{48,16},{1,33},{17,49},{33,1},{49,17},{2,34}... | collective-permute-start | bytes 294920 | tf_op jit(solution)/shard_map/ppermute | solution.py:256
  45.5 7.5 %collective-permute-start.3 = (bf16[1536,256]{1,0:T(8,128)(2,1)S(1)}, bf16[1536,256]{1,0:T(8,128)(2,1)S(1)}, u32[]{:S(2)}, u32[]{:S(2)}) collective-permute-start(bf16[1536,256]{1,0:T(8,128)(2,1)S(1)} %bitcast.3), channel_id=1, source_target_pairs={{0,64},{64,0},{1,65},{65,1},{2,66},{66,2},{3,67},{67,3},{4,68},{68... | collective-permute-start | bytes 2359304 | tf_op jit(solution)/shard_map/ppermute | solution.py:257

commit v5 on v4

--- a/solution.py
+++ b/solution.py
@@ -28,19 +28,27 @@
     return [pl.BlockSpec(memory_space=pltpu.VMEM)] * count
 
 
-def pack_kernel(q_ref, k_ref, v_ref, out_ref, near_ref, done):
+def pack_kernel(q_ref, k_ref, v_ref, out_ref, near_ref, ready_ref, done):
     copies = [
         pltpu.make_async_copy(source, near_ref.at[place], done.at[place])
         for place, source in enumerate((q_ref, k_ref, v_ref))
     ]
     for copy in copies:
         copy.start()
+    sent = []
     for place, copy in enumerate(copies):
         copy.wait()
+        lanes = slice(place * HD, (place + 1) * HD)
         for head in range(HEADS):
-            out_ref[head, :, place * HD : (place + 1) * HD] = near_ref[
-                place, :, head * HD : (head + 1) * HD
-            ]
+            ready_ref[head, :, lanes] = near_ref[place, :, head * HD : (head + 1) * HD]
+        sent.append(
+            pltpu.make_async_copy(
+                ready_ref.at[:, :, lanes], out_ref.at[:, :, lanes], done.at[3 + place]
+            )
+        )
+        sent[-1].start()
+    for copy in sent:
+        copy.wait()
 
 
 def pack(queries, keys, values):
@@ -48,28 +56,28 @@
         pack_kernel,
         out_shape=jax.ShapeDtypeStruct((HEADS, TOKENS, 3 * HD), jnp.bfloat16),
         in_specs=[pl.BlockSpec(memory_space=pl.ANY)] * 3,
-        out_specs=pl.BlockSpec(memory_space=pltpu.VMEM),
+        out_specs=pl.BlockSpec(memory_space=pl.ANY),
         scratch_shapes=[
             pltpu.VMEM((3, TOKENS, HEADS * HD), jnp.bfloat16),
-            pltpu.SemaphoreType.DMA((3,)),
+            pltpu.VMEM((HEADS, TOKENS, 3 * HD), jnp.bfloat16),
+            pltpu.SemaphoreType.DMA((6,)),
         ],
         name="pack",
     )(queries, keys, values)
 
 
-def load_keys(kv_ref, keys_ref, wide_ref):
-    keys_ref[...] = kv_ref[:, :HD]
+def load_values(kv_ref, wide_ref):
     wide_ref[:, :HD] = kv_ref[:, HD:]
     wide_ref[:, HD:] = jnp.ones((kv_ref.shape[0], HD), jnp.bfloat16)
 
 
-def fold(q_refs, keys_ref, wide_ref, scores_ref, rows, finish):
+def fold(q_refs, kv_ref, wide_ref, scores_ref, rows, finish):
     each = q_refs[0].shape[0] // rows
 
     def scores(step):
         return lax.dot_general(
             q_refs[step // each][step % each * rows : (step % each + 1) * rows, :],
-            keys_ref[...],
+            kv_ref[:, :HD],
             (((1,), (1,)), ((), ())),
             preferred_element_type=jnp.float32,
         )
@@ -96,11 +104,11 @@
 
 
 def first_kernel(
-    q0_ref, q1_ref, q2_ref, kv_ref, top_ref, sums_ref, keys_ref, wide_ref, scores_ref, *, rows
+    q0_ref, q1_ref, q2_ref, kv_ref, top_ref, sums_ref, wide_ref, scores_ref, *, rows
 ):
-    load_keys(kv_ref, keys_ref, wide_ref)
+    load_values(kv_ref, wide_ref)
     q_refs = (q0_ref, q1_ref, q2_ref)
-    fold(q_refs, keys_ref, wide_ref, scores_ref, rows, store_state(top_ref, sums_ref, rows))
+    fold(q_refs, kv_ref, wide_ref, scores_ref, rows, store_state(top_ref, sums_ref, rows))
 
 
 def second_kernel(
@@ -114,20 +122,18 @@
     top_ref,
     sums_ref,
     out_ref,
-    keys_ref,
     wide_ref,
     scores_ref,
-    other_keys_ref,
     other_wide_ref,
     last_top_ref,
     last_sums_ref,
     *,
     rows,
 ):
-    load_keys(kv_ref, keys_ref, wide_ref)
-    load_keys(other_ref, other_keys_ref, other_wide_ref)
+    load_values(kv_ref, wide_ref)
+    load_values(other_ref, other_wide_ref)
     last = store_state(last_top_ref, last_sums_ref, rows)
-    fold((q3_ref,), keys_ref, wide_ref, scores_ref, rows, last)
+    fold((q3_ref,), kv_ref, wide_ref, scores_ref, rows, last)
     blocks = rows // TOKENS
     each = HEADS // blocks
     lane = lax.broadcasted_iota(jnp.int32, (blocks, SIDE, HD), 2)
@@ -157,13 +163,12 @@
         ).astype(jnp.bfloat16)
 
     q_refs = (q0_ref, q1_ref, q2_ref, q3_ref)
-    fold(q_refs, other_keys_ref, other_wide_ref, scores_ref, rows, finish)
+    fold(q_refs, other_ref, other_wide_ref, scores_ref, rows, finish)
 
 
 def attend(queries, kv, other_kv, me, rows=192):
     slot, keys = queries[0].shape[0], kv.shape[0]
     scratch = [
-        pltpu.VMEM((keys, HD), jnp.bfloat16),
         pltpu.VMEM((keys, 2 * HD), jnp.bfloat16),
         pltpu.VMEM((2, rows, keys), jnp.float32),
     ]
@@ -188,7 +193,7 @@
         in_specs=whole(6) + [pl.BlockSpec(memory_space=pltpu.SMEM)] + whole(2),
         out_specs=pl.BlockSpec(memory_space=pltpu.VMEM),
         scratch_shapes=scratch
-        + scratch[:2]
+        + scratch[:1]
         + [pltpu.VMEM((slot, HD), jnp.float32), pltpu.VMEM((slot, 2 * HD), jnp.float32)],
         compiler_params=VMEM,
         cost_estimate=pl.CostEstimate(

time: 82 us -> 81.9 us (level)
  no operation moved by 1% of the time
where the time goes in v5:
time: 81.9 us; the launch traced here: 81.5 us
  blocking collectives  44.7 us (55%)
  starting transfers between devices  23 us (28%)
  Pallas kernels  9.72 us (12%)
  waiting for transfers between devices  3.05 us (4%)
  local copies, waits for them, and re-layouts  0.97 us (1%)
    all_to_all x1, blocking collectives, per_device(): lax.all_to_all(parts, BACK_GROUP, split_axis=0, concat_axis=0, tiled=True)  23 us
    all_to_all x1, blocking collectives, per_device(): lax.all_to_all(packed, HEAD_GROUP, split_axis=0, concat_axis=0, tiled=True)  21.7 us
    ppermute x3, starting transfers between devices, per_device(): query = [own_q] + [lax.ppermute(own_q, 'zh', swap(by)) for by in TURNS[1:]]  16.2 us
    all_to_all x1, starting transfers between devices, spread(): lax.all_to_all(copies, axis, split_axis=0, concat_axis=0, tiled=True)  4.82 us
    pallas_call x1, Pallas kernels, attend(): pl.pallas_call(functools.partial(second_kernel, rows=rows), out_shape=jax...  4.21 us
    ppermute x3, waiting for transfers between devices, per_device(): query = [own_q] + [lax.ppermute(own_q, 'zh', swap(by)) for by in TURNS[1:]]  3.05 us
    pallas_call x1, Pallas kernels, attend(): pl.pallas_call(functools.partial(first_kernel, rows=rows), out_shape=[jax...  2.47 us
    ppermute x1, starting transfers between devices, per_device(): other_kv = lax.ppermute(kv, 'c', [(0, 1), (1, 0)])  1.92 us
  transfers between devices with their start and end apart: 5, of which 2 were waited for; matrix products, arithmetic and copies ran while one was open for 0% of the time, Pallas kernels for 3%

profile of v5, /device:TPU:2, one launch (start us, length us, event | category | flops | bytes accessed | tf_op | source)
XLA Modules:
  0.0 81.5 jit_solution(3693680522489791048)
XLA Ops:
  0.0 1.7 %pack.1 = bf16[16,24,384]{2,1,0:T(8,128)(2,1)} custom-call(bf16[24,2048]{1,0:T(8,128)(2,1)} %q_ref.1, bf16[24,2048]{1,0:T(8,128)(2,1)} %k_ref.1, bf16[24,2048]{1,0:T(8,128)(2,1)} %v_ref.1), custom_call_target="tpu_custom_call" | custom-call | tf_op jit(solution)/shard_map/pack/pallas_call | solution.py:55
  1.7 21.7 %all_to_all.15 = bf16[16,24,384]{2,1,0:T(8,128)(2,1)S(1)} all-to-all(bf16[16,24,384]{2,1,0:T(8,128)(2,1)} %pack.1), channel_id=1, replica_groups=mesh['yl'=4,'c'=2,'zh'=4,'zl'=2,'x'=4,'yh'=2] {'yh','yl','zl'}, dimensions={0} | all-to-all | bytes 589824 | tf_op jit(solution)/shard_map/all_to_all | solution.py:257
  23.4 0.9 %broadcast_in_dim.2 = bf16[4,384,256]{2,1,0:T(8,128)(2,1)} broadcast(bf16[384,256]{1,0:T(8,128)(2,1)S(1)} %slice.9), dimensions={1,2} | broadcast | bytes 983040 | tf_op jit(solution)/shard_map/broadcast_in_dim | solution.py:246
  24.3 4.8 %all-to-all-start.1 = ((bf16[4,384,256]{2,1,0:T(8,128)(2,1)}), bf16[4,384,256]{2,1,0:T(8,128)(2,1)S(1)}, u32[]{:S(2)}, u32[]{:S(2)}) async-start(bf16[4,384,256]{2,1,0:T(8,128)(2,1)} %broadcast_in_dim.2), calls=%async_computation.1 | async-start | bytes 1572864 | tf_op jit(solution)/shard_map/all_to_all | solution.py:247
  29.2 10.0 %collective-permute-start.1 = (bf16[384,128]{1,0:T(8,128)(2,1)S(1)}, bf16[384,128]{1,0:T(8,128)(2,1)S(1)}, u32[]{:S(2)}, u32[]{:S(2)}) collective-permute-start(bf16[384,128]{1,0:T(8,128)(2,1)S(1)} %slice.8.q0_ref), channel_id=1, source_target_pairs={{0,48},{16,32},{32,16},{48,0},{1,49},{17,33},{33,17},{49,1},{2,50}... | collective-permute-start | bytes 294920 | tf_op jit(solution)/shard_map/ppermute | solution.py:261
  39.2 2.5 %collective-permute-start = (bf16[384,128]{1,0:T(8,128)(2,1)S(1)}, bf16[384,128]{1,0:T(8,128)(2,1)S(1)}, u32[]{:S(2)}, u32[]{:S(2)}) collective-permute-start(bf16[384,128]{1,0:T(8,128)(2,1)S(1)} %slice.8.q0_ref), channel_id=1, source_target_pairs={{0,16},{16,0},{32,48},{48,32},{1,17},{17,1},{33,49},{49,33},{2,18}... | collective-permute-start | bytes 294920 | tf_op jit(solution)/shard_map/ppermute | solution.py:261
  41.7 3.7 %collective-permute-start.2 = (bf16[384,128]{1,0:T(8,128)(2,1)S(1)}, bf16[384,128]{1,0:T(8,128)(2,1)S(1)}, u32[]{:S(2)}, u32[]{:S(2)}) collective-permute-start(bf16[384,128]{1,0:T(8,128)(2,1)S(1)} %slice.8.q0_ref), channel_id=1, source_target_pairs={{0,32},{16,48},{32,0},{48,16},{1,33},{17,49},{33,1},{49,17},{2,34}... | collective-permute-start | bytes 294920 | tf_op jit(solution)/shard_map/ppermute | solution.py:261
  45.4 0.0 all-to-all-done.1
  45.4 1.9 %collective-permute-start.3 = (bf16[1536,256]{1,0:T(8,128)(2,1)S(1)}, bf16[1536,256]{1,0:T(8,128)(2,1)S(1)}, u32[]{:S(2)}, u32[]{:S(2)}) collective-permute-start(bf16[1536,256]{1,0:T(8,128)(2,1)S(1)} %bitcast.3), channel_id=1, source_target_pairs={{0,64},{64,0},{1,65},{65,1},{2,66},{66,2},{3,67},{67,3},{4,68},{68... | collective-permute-start | bytes 2359304 | tf_op jit(solution)/shard_map/ppermute | solution.py:262
  47.4 0.0 collective-permute-done.1.q2_ref
  47.4 2.4 %collective-permute-done.q1_ref = bf16[384,128]{1,0:T(8,128)(2,1)S(1)} collective-permute-done((bf16[384,128]{1,0:T(8,128)(2,1)S(1)}, bf16[384,128]{1,0:T(8,128)(2,1)S(1)}, u32[]{:S(2)}, u32[]{:S(2)}) %collective-permute-start) | collective-permute-done | bytes 98336 | tf_op jit(solution)/shard_map/ppermute | solution.py:261
  49.8 2.5 %attend_first.1 = (f32[1152,128]{1,0:T(8,128)S(1)}, f32[1152,256]{1,0:T(8,128)S(1)}) custom-call(bf16[384,128]{1,0:T(8,128)(2,1)S(1)} %slice.8.q0_ref, bf16[384,128]{1,0:T(8,128)(2,1)S(1)} %collective-permute-done.q1_ref, bf16[384,128]{1,0:T(8,128)(2,1)S(1)} %collective-permute-done.1.q2_ref, bf16[1536,256]{1,0:T(8,128)(2,1)S(1)} %bitcast.4), custom_call_target="tpu_custom_call" | custom-call | flops 14495514624 | bytes 4194304 | tf_op jit(solution)/shard_map/attend_first/pallas_call | solution.py:175
  52.3 0.6 collective-permute-done.2.q3_ref
  52.9 0.0 collective-permute-done.3.other_ref
  52.9 4.2 %attend_second.1 = bf16[64,32,128]{2,1,0:T(8,128)(2,1)S(1)} custom-call(bf16[384,128]{1,0:T(8,128)(2,1)S(1)} %slice.8.q0_ref, bf16[384,128]{1,0:T(8,128)(2,1)S(1)} %collective-permute-done.q1_ref, bf16[384,128]{1,0:T(8,128)(2,1)S(1)} %collective-permute-done.1.q2_ref, bf16[384,128]{1,0:T(8,128)(2,1)S(1)} %collective-permute-done.2.q3_ref, ...), custom_call_target="tpu_custom_call" | custom-call | flops 3019898880 | bytes 4194304 | tf_op jit(solution)/shard_map/attend_second/pallas_call | solution.py:190
  57.1 23.0 %all_to_all.16.parts_ref = bf16[64,32,128]{2,1,0:T(8,128)(2,1)S(1)} all-to-all(bf16[64,32,128]{2,1,0:T(8,128)(2,1)S(1)} %attend_second.1), channel_id=1, replica_groups=mesh['yl'=4,'c'=2,'zh'=4,'zl'=2,'x'=4,'yh'=2] {'zh','yh','yl','zl'}, dimensions={0} | all-to-all | bytes 1048576 | tf_op jit(solution)/shard_map/all_to_all | solution.py:265
  80.1 1.4 %combine.1 = bf16[24,2048]{1,0:T(8,128)(2,1)} custom-call(bf16[64,32,128]{2,1,0:T(8,128)(2,1)S(1)} %all_to_all.16.parts_ref), custom_call_target="tpu_custom_call" | custom-call | tf_op jit(solution)/shard_map/combine/pallas_call | solution.py:235
  (2 shorter events, 0.0 us)
Async XLA Ops:
  24.3 21.1 %all-to-all-start.1 = ((bf16[4,384,256]{2,1,0:T(8,128)(2,1)}), bf16[4,384,256]{2,1,0:T(8,128)(2,1)S(1)}, u32[]{:S(2)}, u32[]{:S(2)}) async-start(bf16[4,384,256]{2,1,0:T(8,128)(2,1)} %broadcast_in_dim.2), calls=%async_computation.1 | async-start | bytes 1572864 | tf_op jit(solution)/shard_map/all_to_all | solution.py:247
  29.2 18.2 %collective-permute-start.1 = (bf16[384,128]{1,0:T(8,128)(2,1)S(1)}, bf16[384,128]{1,0:T(8,128)(2,1)S(1)}, u32[]{:S(2)}, u32[]{:S(2)}) collective-permute-start(bf16[384,128]{1,0:T(8,128)(2,1)S(1)} %slice.8.q0_ref), channel_id=1, source_target_pairs={{0,48},{16,32},{32,16},{48,0},{1,49},{17,33},{33,17},{49,1},{2,50}... | collective-permute-start | bytes 294920 | tf_op jit(solution)/shard_map/ppermute | solution.py:261
  39.2 10.6 %collective-permute-start = (bf16[384,128]{1,0:T(8,128)(2,1)S(1)}, bf16[384,128]{1,0:T(8,128)(2,1)S(1)}, u32[]{:S(2)}, u32[]{:S(2)}) collective-permute-start(bf16[384,128]{1,0:T(8,128)(2,1)S(1)} %slice.8.q0_ref), channel_id=1, source_target_pairs={{0,16},{16,0},{32,48},{48,32},{1,17},{17,1},{33,49},{49,33},{2,18}... | collective-permute-start | bytes 294920 | tf_op jit(solution)/shard_map/ppermute | solution.py:261
  41.7 11.2 %collective-permute-start.2 = (bf16[384,128]{1,0:T(8,128)(2,1)S(1)}, bf16[384,128]{1,0:T(8,128)(2,1)S(1)}, u32[]{:S(2)}, u32[]{:S(2)}) collective-permute-start(bf16[384,128]{1,0:T(8,128)(2,1)S(1)} %slice.8.q0_ref), channel_id=1, source_target_pairs={{0,32},{16,48},{32,0},{48,16},{1,33},{17,49},{33,1},{49,17},{2,34}... | collective-permute-start | bytes 294920 | tf_op jit(solution)/shard_map/ppermute | solution.py:261
  45.4 7.5 %collective-permute-start.3 = (bf16[1536,256]{1,0:T(8,128)(2,1)S(1)}, bf16[1536,256]{1,0:T(8,128)(2,1)S(1)}, u32[]{:S(2)}, u32[]{:S(2)}) collective-permute-start(bf16[1536,256]{1,0:T(8,128)(2,1)S(1)} %bitcast.3), channel_id=1, source_target_pairs={{0,64},{64,0},{1,65},{65,1},{2,66},{66,2},{3,67},{67,3},{4,68},{68... | collective-permute-start | bytes 2359304 | tf_op jit(solution)/shard_map/ppermute | solution.py:262

commit v6 on v5

--- a/solution.py
+++ b/solution.py
@@ -242,10 +242,29 @@
     )(parts)
 
 
-def spread(array, axis, size):
-    copies = jnp.broadcast_to(array[None], (size,) + array.shape)
-    gathered = lax.all_to_all(copies, axis, split_axis=0, concat_axis=0, tiled=True)
-    return gathered.reshape(size * array.shape[0], array.shape[1])
+def copies_kernel(in_ref, out_ref, done):
+    copies = [
+        pltpu.make_async_copy(in_ref.at[:, HD:], out_ref.at[member], done.at[member])
+        for member in range(4)
+    ]
+    for copy in copies:
+        copy.start()
+    for copy in copies:
+        copy.wait()
+
+
+def spread(mine):
+    copies = pl.pallas_call(
+        copies_kernel,
+        out_shape=jax.ShapeDtypeStruct((4, mine.shape[0], 2 * HD), jnp.bfloat16),
+        in_specs=whole(1),
+        out_specs=pl.BlockSpec(memory_space=pl.ANY),
+        scratch_shapes=[pltpu.SemaphoreType.DMA((4,))],
+        compiler_params=VMEM,
+        name="copies",
+    )(mine)
+    gathered = lax.all_to_all(copies, "x", split_axis=0, concat_axis=0, tiled=True)
+    return gathered.reshape(4 * mine.shape[0], 2 * HD)
 
 
 def swap(by):
@@ -257,7 +276,7 @@
     mine = lax.all_to_all(packed, HEAD_GROUP, split_axis=0, concat_axis=0, tiled=True)
     mine = mine.reshape(HEADS * TOKENS, 3 * HD)
     own_q = mine[:, :HD]
-    kv = spread(mine[:, HD:], "x", 4)
+    kv = spread(mine)
     query = [own_q] + [lax.ppermute(own_q, "zh", swap(by)) for by in TURNS[1:]]
     other_kv = lax.ppermute(kv, "c", [(0, 1), (1, 0)])
     me = lax.axis_index("zh").astype(jnp.int32).reshape(1)

time: 81.9 us -> 81.9 us (level)
  Pallas kernels: 9.72 us -> 10.7 us
  local copies, waits for them, and re-layouts: 0.97 us -> 0.01 us
    broadcast_in_dim x1 -> x0, local copies, waits for them, and re-layouts: 0.94 us -> none  [spread(): copies = jnp.broadcast_to(array[None], (size,) + array.shape)]
    pallas_call x0 -> x1, Pallas kernels: none -> 0.93 us  [spread(): pl.pallas_call(copies_kernel, out_shape=jax.ShapeDtypeStruct((4, mine.sha...]
where the time goes in v6:
time: 81.9 us; the launch traced here: 81.5 us
  blocking collectives  44.7 us (55%)
  starting transfers between devices  23 us (28%)
  Pallas kernels  10.7 us (13%)
  waiting for transfers between devices  3.05 us (4%)
    all_to_all x1, blocking collectives, per_device(): lax.all_to_all(parts, BACK_GROUP, split_axis=0, concat_axis=0, tiled=True)  23 us
    all_to_all x1, blocking collectives, per_device(): lax.all_to_all(packed, HEAD_GROUP, split_axis=0, concat_axis=0, tiled=True)  21.7 us
    ppermute x3, starting transfers between devices, per_device(): query = [own_q] + [lax.ppermute(own_q, 'zh', swap(by)) for by in TURNS[1:]]  16.2 us
    all_to_all x1, starting transfers between devices, spread(): lax.all_to_all(copies, 'x', split_axis=0, concat_axis=0, tiled=True)  4.84 us
    pallas_call x1, Pallas kernels, attend(): pl.pallas_call(functools.partial(second_kernel, rows=rows), out_shape=jax...  4.21 us
    ppermute x3, waiting for transfers between devices, per_device(): query = [own_q] + [lax.ppermute(own_q, 'zh', swap(by)) for by in TURNS[1:]]  3.05 us
    pallas_call x1, Pallas kernels, attend(): pl.pallas_call(functools.partial(first_kernel, rows=rows), out_shape=[jax...  2.47 us
    ppermute x1, starting transfers between devices, per_device(): other_kv = lax.ppermute(kv, 'c', [(0, 1), (1, 0)])  1.92 us
  transfers between devices with their start and end apart: 5, of which 2 were waited for; matrix products, arithmetic and copies ran while one was open for 0% of the time, Pallas kernels for 3%

profile of v6, /device:TPU:2, one launch (start us, length us, event | category | flops | bytes accessed | tf_op | source)
XLA Modules:
  0.0 81.5 jit_solution(9282416674683357822)
XLA Ops:
  0.0 1.7 %pack.1 = bf16[16,24,384]{2,1,0:T(8,128)(2,1)} custom-call(bf16[24,2048]{1,0:T(8,128)(2,1)} %q_ref.1, bf16[24,2048]{1,0:T(8,128)(2,1)} %k_ref.1, bf16[24,2048]{1,0:T(8,128)(2,1)} %v_ref.1), custom_call_target="tpu_custom_call" | custom-call | tf_op jit(solution)/shard_map/pack/pallas_call | solution.py:55
  1.7 21.7 %all_to_all.15 = bf16[16,24,384]{2,1,0:T(8,128)(2,1)S(1)} all-to-all(bf16[16,24,384]{2,1,0:T(8,128)(2,1)} %pack.1), channel_id=1, replica_groups=mesh['yl'=4,'c'=2,'zh'=4,'zl'=2,'x'=4,'yh'=2] {'yh','yl','zl'}, dimensions={0} | all-to-all | bytes 589824 | tf_op jit(solution)/shard_map/all_to_all | solution.py:276
  23.4 0.9 %copies.1 = bf16[4,384,256]{2,1,0:T(8,128)(2,1)} custom-call(bf16[384,384]{1,0:T(8,128)(2,1)S(1)} %bitcast.3), custom_call_target="tpu_custom_call" | custom-call | tf_op jit(solution)/shard_map/copies/pallas_call | solution.py:257
  24.3 4.8 %all-to-all-start.1 = ((bf16[4,384,256]{2,1,0:T(8,128)(2,1)}), bf16[4,384,256]{2,1,0:T(8,128)(2,1)S(1)}, u32[]{:S(2)}, u32[]{:S(2)}) async-start(bf16[4,384,256]{2,1,0:T(8,128)(2,1)} %copies.1), calls=%async_computation.1 | async-start | bytes 1572864 | tf_op jit(solution)/shard_map/all_to_all | solution.py:266
  29.2 10.0 %collective-permute-start.1 = (bf16[384,128]{1,0:T(8,128)(2,1)S(1)}, bf16[384,128]{1,0:T(8,128)(2,1)S(1)}, u32[]{:S(2)}, u32[]{:S(2)}) collective-permute-start(bf16[384,128]{1,0:T(8,128)(2,1)S(1)} %slice.4.q0_ref), channel_id=1, source_target_pairs={{0,48},{16,32},{32,16},{48,0},{1,49},{17,33},{33,17},{49,1},{2,50}... | collective-permute-start | bytes 294920 | tf_op jit(solution)/shard_map/ppermute | solution.py:280
  39.2 2.5 %collective-permute-start = (bf16[384,128]{1,0:T(8,128)(2,1)S(1)}, bf16[384,128]{1,0:T(8,128)(2,1)S(1)}, u32[]{:S(2)}, u32[]{:S(2)}) collective-permute-start(bf16[384,128]{1,0:T(8,128)(2,1)S(1)} %slice.4.q0_ref), channel_id=1, source_target_pairs={{0,16},{16,0},{32,48},{48,32},{1,17},{17,1},{33,49},{49,33},{2,18}... | collective-permute-start | bytes 294920 | tf_op jit(solution)/shard_map/ppermute | solution.py:280
  41.7 3.7 %collective-permute-start.2 = (bf16[384,128]{1,0:T(8,128)(2,1)S(1)}, bf16[384,128]{1,0:T(8,128)(2,1)S(1)}, u32[]{:S(2)}, u32[]{:S(2)}) collective-permute-start(bf16[384,128]{1,0:T(8,128)(2,1)S(1)} %slice.4.q0_ref), channel_id=1, source_target_pairs={{0,32},{16,48},{32,0},{48,16},{1,33},{17,49},{33,1},{49,17},{2,34}... | collective-permute-start | bytes 294920 | tf_op jit(solution)/shard_map/ppermute | solution.py:280
  45.4 0.0 all-to-all-done.1
  45.4 1.9 %collective-permute-start.3 = (bf16[1536,256]{1,0:T(8,128)(2,1)S(1)}, bf16[1536,256]{1,0:T(8,128)(2,1)S(1)}, u32[]{:S(2)}, u32[]{:S(2)}) collective-permute-start(bf16[1536,256]{1,0:T(8,128)(2,1)S(1)} %bitcast.5), channel_id=1, source_target_pairs={{0,64},{64,0},{1,65},{65,1},{2,66},{66,2},{3,67},{67,3},{4,68},{68... | collective-permute-start | bytes 2359304 | tf_op jit(solution)/shard_map/ppermute | solution.py:281
  47.3 0.0 collective-permute-done.1.q2_ref
  47.4 2.4 %collective-permute-done.q1_ref = bf16[384,128]{1,0:T(8,128)(2,1)S(1)} collective-permute-done((bf16[384,128]{1,0:T(8,128)(2,1)S(1)}, bf16[384,128]{1,0:T(8,128)(2,1)S(1)}, u32[]{:S(2)}, u32[]{:S(2)}) %collective-permute-start) | collective-permute-done | bytes 98336 | tf_op jit(solution)/shard_map/ppermute | solution.py:280
  49.8 2.5 %attend_first.1 = (f32[1152,128]{1,0:T(8,128)S(1)}, f32[1152,256]{1,0:T(8,128)S(1)}) custom-call(bf16[384,128]{1,0:T(8,128)(2,1)S(1)} %slice.4.q0_ref, bf16[384,128]{1,0:T(8,128)(2,1)S(1)} %collective-permute-done.q1_ref, bf16[384,128]{1,0:T(8,128)(2,1)S(1)} %collective-permute-done.1.q2_ref, bf16[1536,256]{1,0:T(8,128)(2,1)S(1)} %bitcast.6), custom_call_target="tpu_custom_call" | custom-call | flops 14495514624 | bytes 4194304 | tf_op jit(solution)/shard_map/attend_first/pallas_call | solution.py:175
  52.3 0.6 collective-permute-done.2.q3_ref
  52.9 0.0 collective-permute-done.3.other_ref
  52.9 4.2 %attend_second.1 = bf16[64,32,128]{2,1,0:T(8,128)(2,1)S(1)} custom-call(bf16[384,128]{1,0:T(8,128)(2,1)S(1)} %slice.4.q0_ref, bf16[384,128]{1,0:T(8,128)(2,1)S(1)} %collective-permute-done.q1_ref, bf16[384,128]{1,0:T(8,128)(2,1)S(1)} %collective-permute-done.1.q2_ref, bf16[384,128]{1,0:T(8,128)(2,1)S(1)} %collective-permute-done.2.q3_ref, ...), custom_call_target="tpu_custom_call" | custom-call | flops 3019898880 | bytes 4194304 | tf_op jit(solution)/shard_map/attend_second/pallas_call | solution.py:190
  57.1 23.0 %all_to_all.16.parts_ref = bf16[64,32,128]{2,1,0:T(8,128)(2,1)S(1)} all-to-all(bf16[64,32,128]{2,1,0:T(8,128)(2,1)S(1)} %attend_second.1), channel_id=1, replica_groups=mesh['yl'=4,'c'=2,'zh'=4,'zl'=2,'x'=4,'yh'=2] {'zh','yh','yl','zl'}, dimensions={0} | all-to-all | bytes 1048576 | tf_op jit(solution)/shard_map/all_to_all | solution.py:284
  80.1 1.4 %combine.1 = bf16[24,2048]{1,0:T(8,128)(2,1)} custom-call(bf16[64,32,128]{2,1,0:T(8,128)(2,1)S(1)} %all_to_all.16.parts_ref), custom_call_target="tpu_custom_call" | custom-call | tf_op jit(solution)/shard_map/combine/pallas_call | solution.py:235
  (1 shorter events, 0.0 us)
Async XLA Ops:
  24.3 21.1 %all-to-all-start.1 = ((bf16[4,384,256]{2,1,0:T(8,128)(2,1)}), bf16[4,384,256]{2,1,0:T(8,128)(2,1)S(1)}, u32[]{:S(2)}, u32[]{:S(2)}) async-start(bf16[4,384,256]{2,1,0:T(8,128)(2,1)} %copies.1), calls=%async_computation.1 | async-start | bytes 1572864 | tf_op jit(solution)/shard_map/all_to_all | solution.py:266
  29.2 18.2 %collective-permute-start.1 = (bf16[384,128]{1,0:T(8,128)(2,1)S(1)}, bf16[384,128]{1,0:T(8,128)(2,1)S(1)}, u32[]{:S(2)}, u32[]{:S(2)}) collective-permute-start(bf16[384,128]{1,0:T(8,128)(2,1)S(1)} %slice.4.q0_ref), channel_id=1, source_target_pairs={{0,48},{16,32},{32,16},{48,0},{1,49},{17,33},{33,17},{49,1},{2,50}... | collective-permute-start | bytes 294920 | tf_op jit(solution)/shard_map/ppermute | solution.py:280
  39.2 10.6 %collective-permute-start = (bf16[384,128]{1,0:T(8,128)(2,1)S(1)}, bf16[384,128]{1,0:T(8,128)(2,1)S(1)}, u32[]{:S(2)}, u32[]{:S(2)}) collective-permute-start(bf16[384,128]{1,0:T(8,128)(2,1)S(1)} %slice.4.q0_ref), channel_id=1, source_target_pairs={{0,16},{16,0},{32,48},{48,32},{1,17},{17,1},{33,49},{49,33},{2,18}... | collective-permute-start | bytes 294920 | tf_op jit(solution)/shard_map/ppermute | solution.py:280
  41.7 11.2 %collective-permute-start.2 = (bf16[384,128]{1,0:T(8,128)(2,1)S(1)}, bf16[384,128]{1,0:T(8,128)(2,1)S(1)}, u32[]{:S(2)}, u32[]{:S(2)}) collective-permute-start(bf16[384,128]{1,0:T(8,128)(2,1)S(1)} %slice.4.q0_ref), channel_id=1, source_target_pairs={{0,32},{16,48},{32,0},{48,16},{1,33},{17,49},{33,1},{49,17},{2,34}... | collective-permute-start | bytes 294920 | tf_op jit(solution)/shard_map/ppermute | solution.py:280
  45.4 7.5 %collective-permute-start.3 = (bf16[1536,256]{1,0:T(8,128)(2,1)S(1)}, bf16[1536,256]{1,0:T(8,128)(2,1)S(1)}, u32[]{:S(2)}, u32[]{:S(2)}) collective-permute-start(bf16[1536,256]{1,0:T(8,128)(2,1)S(1)} %bitcast.5), channel_id=1, source_target_pairs={{0,64},{64,0},{1,65},{65,1},{2,66},{66,2},{3,67},{67,3},{4,68},{68... | collective-permute-start | bytes 2359304 | tf_op jit(solution)/shard_map/ppermute | solution.py:281
